TPU v7x, 128 devices: a whole 4x4x4 slice. The times are simulated.
128 devices in a mesh: pair: 2 (over x_hi), day: 16 (over z, y), lag: 4 (over x_lo, core).
Axes of the slice: x: 4 (x_hi: 2, x_lo: 2; x = x_hi * 2 + x_lo), y: 4, z: 4, core: 2. Of those that a mesh axis runs over, the one named last changes fastest.
Arguments:
- corr: bfloat16 [2048, 64, 2048], P('pair', 'day', 'lag'), may hold values from -150 to 150
Outputs:
- pws_stack: float32 [2048, 2048], P('pair', 'lag')
- robust_stack: float32 [2048, 2048], P('pair', 'lag')
- day_weights: float32 [2048, 64], P('pair', 'day')
All inputs are finite; a program needn't handle non-finite values.
Results may differ from a plain program's by a relative error of at most 0.00049.
Values may be sent and summed in bfloat16 or wider, within the bound.
A program may use at most 128 MiB of HBM per device.

v0:
```python
import jax
import jax.numpy as jnp
from jax import lax
from jax.sharding import PartitionSpec as P

ITERS = 3


epsilon = 1e-06


def kernel_block(rows, cols, lags):
    offset = (cols[None, :] - rows[:, None]) % lags
    odd = offset % 2 == 1
    angle = jnp.pi * offset.astype(jnp.float32) / lags
    value = jnp.where(odd, 2.0 / lags * jnp.cos(angle) / jnp.where(odd, jnp.sin(angle), 1.0), 0.0)
    return value.astype(jnp.bfloat16)


def per_device(corr):
    width_in = corr.shape[2]
    lags = width_in * lax.axis_size("lag")
    pairs, days_here, width = corr.shape
    days = days_here * lax.axis_size("day")
    data = corr.astype(jnp.float32)
    squares = jnp.sum(data * data, axis=2)
    norm2 = lax.psum(squares, "lag")
    rms = jnp.sqrt(norm2 / lags + epsilon)
    xn = data / rms[:, :, None]
    local_lags = lax.axis_index("lag") * width + jnp.arange(width, dtype=jnp.int32)
    piece = lax.all_gather(corr, "lag", axis=2, tiled=True)
    count = piece.shape[2]
    rows = jnp.arange(count, dtype=jnp.int32)
    block = kernel_block(rows, local_lags, lags)
    quad = jnp.dot(
        piece.reshape(pairs * days_here, count), block, preferred_element_type=jnp.float32
    )
    quad = quad.reshape(pairs, days_here, width)
    den = jnp.maximum(jnp.sqrt(data * data + quad * quad), 0.1 * rms[:, :, None])
    cosine = data / den
    sine = quad / den
    linear, csum, ssum = lax.psum(
        (jnp.sum(xn, axis=1), jnp.sum(cosine, axis=1), jnp.sum(sine, axis=1)), "day"
    )
    pws = linear / days * ((csum * csum + ssum * ssum) / (days * days))
    stack = pws
    for step in range(ITERS):
        energy = jnp.sum(stack * stack, axis=1)
        msq = lax.psum(energy, "lag") / lags
        normed = stack / jnp.sqrt(msq + epsilon)[:, None]
        inner = jnp.sum(xn * normed[:, None, :], axis=2)
        coh = lax.psum(inner, "lag") / lags
        spread = jnp.sum((xn - coh[:, :, None] * normed[:, None, :]) ** 2, axis=2)
        res = lax.psum(spread, "lag") / lags
        rbar = lax.psum(jnp.sum(res, axis=1), "day") / days
        weight = (0.1 + jnp.abs(coh)) / (res + rbar[:, None] + epsilon)
        stack, total = lax.psum(
            (jnp.sum(weight[:, :, None] * xn, axis=1), jnp.sum(weight, axis=1)), "day"
        )
    robust = stack / total[:, None]
    shares = weight / total[:, None]
    return (pws, robust, shares)


def solution(mesh):
    return jax.shard_map(
        per_device,
        mesh=mesh,
        in_specs=(P("pair", "day", "lag"),),
        out_specs=(P("pair", "lag"), P("pair", "lag"), P("pair", "day")),
        check_vma=False,
    )
```

profile of v0, /device:TPU:1, one launch (start us, length us, event | category | flops | bytes accessed | tf_op | source)
XLA Modules:
  0.0 961.3 jit_solution(4867787955644400862)
XLA Ops:
  12.4 16.9 %psum.140 = f32[1024,4]{1,0:T(8,128)S(1)} all-reduce(f32[1024,4]{1,0:T(8,128)S(1)} %fusion.1), channel_id=1, replica_groups=mesh['pair'=2,'day'=16,'lag'=4] {'lag'}, use_global_device_ids=true, to_apply=%region_1.0 | all-reduce | flops 4096 | bytes 32768 | tf_op jit(solution)/shard_map/psum | solution.py:27
  29.5 19.0 %select_convert_fusion.4 = bf16[2048,512]{1,0:T(8,128)(2,1)S(1)} fusion(s32[512]{0:T(512)S(1)} %iota_add_fusion), kind=kLoop, calls=%fused_computation.28.clone.clone.1 | loop fusion | flops 32505856 | bytes 2099200 | tf_op jit(solution)/shard_map/dot_general | solution.py:35
  48.5 116.2 %all-gather.2.cloned.1.call-done = bf16[1024,4,2048]{2,1,0:T(4,128)(2,1)} async-done(((bf16[1024,4,512]{2,1,0:T(4,128)(2,1)}), bf16[1024,4,2048]{2,1,0:T(4,128)(2,1)}) %all-gather.2.cloned.1.call-update) | async-done | bytes 16777232 | tf_op jit(solution)/shard_map/all_gather | solution.py:31
  164.7 23.7 %reshape.35 = bf16[4096,2048]{1,0:T(8,128)(2,1)} reshape(bf16[1024,4,2048]{2,1,0:T(4,128)(2,1)} %all-gather.2.cloned.1.call-done) | data formatting | bytes 33554432 | tf_op jit(solution)/shard_map/reshape | solution.py:36
  188.3 14.5 %convolution_bitcast_fusion = f32[4096,512]{0,1:T(8,128)} fusion(bf16[4096,2048]{1,0:T(8,128)(2,1)} %reshape.35, bf16[2048,512]{1,0:T(8,128)(2,1)S(1)} %select_convert_fusion.4), kind=kOutput, calls=%fused_computation.18 | convolution fusion | flops 8589934592 | bytes 27262976 | tf_op jit(solution)/shard_map/dot_general | solution.py:35
  211.9 9.8 %reshape.36 = f32[1024,4,512]{2,1,0:T(4,128)} reshape(f32[4096,512]{1,0:T(8,128)} %copy.24) | data formatting | bytes 16777216 | tf_op jit(solution)/shard_map/reshape | solution.py:38
  221.7 32.9 %fusion.34 = (f32[1024,512]{1,0:T(8,128)}, f32[1024,4,512]{2,1,0:T(4,128)}, f32[1024,512]{1,0:T(8,128)}, f32[1024,512]{1,0:T(8,128)}) fusion(f32[1024,4]{1,0:T(8,128)S(1)} %get-tuple-element.19, bf16[1024,4,512]{2,1,0:T(4,128)(2,1)} %param.1, f32[1024,4,512]{2,1,0:T(4,128)} %reshape.36, f32[1024,4]{1,0:T(8,128)S(1)} %get-tuple-element.20), kind=kLoop, calls=%fused_computation.82 | loop fusion | flops 21495808 | bytes 27295744 | tf_op jit(solution)/shard_map/reduce_sum | solution.py:43
  254.7 124.3 %all-reduce.12.cloned.1.call-done = (f32[1024,512]{1,0:T(8,128)}, f32[1024,512]{1,0:T(8,128)}, f32[1024,512]{1,0:T(8,128)}) async-done(((f32[1024,512]{1,0:T(8,128)}, f32[1024,512]{1,0:T(8,128)}, f32[1024,512]{1,0:T(8,128)}), (f32[1024,512]{1,0:T(8,128)}, f32[1024,512]{1,0:T(8,128)}, f32[1024,512]{1,0:T(8,128)})) %all-reduce.12.cloned.1.call-update) | async-done | bytes 6291472 | tf_op jit(solution)/shard_map/psum | solution.py:42
  396.9 16.1 %psum.145 = f32[1024,4]{1,0:T(8,128)S(1)} all-reduce(f32[1024,4]{1,0:T(8,128)S(1)} %multiply_reduce_fusion.8), channel_id=1, replica_groups=mesh['pair'=2,'day'=16,'lag'=4] {'lag'}, use_global_device_ids=true, to_apply=%region_11.12 | all-reduce | flops 4096 | bytes 32768 | tf_op jit(solution)/shard_map/psum | solution.py:52
  420.1 16.3 %psum.146 = f32[1024,4]{1,0:T(8,128)S(1)} all-reduce(f32[1024,4]{1,0:T(8,128)S(1)} %multiply_reduce_fusion.7), channel_id=1, replica_groups=mesh['pair'=2,'day'=16,'lag'=4] {'lag'}, use_global_device_ids=true, to_apply=%region_13.14 | all-reduce | flops 4096 | bytes 32768 | tf_op jit(solution)/shard_map/psum | solution.py:54
  436.6 31.3 %psum.147 = f32[1024]{0:T(1024)S(1)} all-reduce(f32[1024]{0:T(1024)S(1)} %multiply_reduce_fusion.14), channel_id=1, replica_groups=mesh['pair'=2,'day'=16,'lag'=4] {'day'}, use_global_device_ids=true, to_apply=%region_15.16 | all-reduce | flops 1024 | bytes 8192 | tf_op jit(solution)/shard_map/psum | solution.py:55
  468.2 9.3 multiply_reduce_fusion.6
  477.6 93.4 %all-reduce.6.cloned.1.call-done = f32[1024,512]{1,0:T(8,128)} async-done(((f32[1024,512]{1,0:T(8,128)}), f32[1024,512]{1,0:T(8,128)}) %all-reduce.6.cloned.1.call-update) | async-done | bytes 2097168 | tf_op jit(solution)/shard_map/psum | solution.py:57
  587.2 16.1 %psum.150 = f32[1024,4]{1,0:T(8,128)S(1)} all-reduce(f32[1024,4]{1,0:T(8,128)S(1)} %multiply_reduce_fusion.5), channel_id=1, replica_groups=mesh['pair'=2,'day'=16,'lag'=4] {'lag'}, use_global_device_ids=true, to_apply=%region_21.22 | all-reduce | flops 4096 | bytes 32768 | tf_op jit(solution)/shard_map/psum | solution.py:52
  610.5 15.9 %psum.151 = f32[1024,4]{1,0:T(8,128)S(1)} all-reduce(f32[1024,4]{1,0:T(8,128)S(1)} %multiply_reduce_fusion.4), channel_id=1, replica_groups=mesh['pair'=2,'day'=16,'lag'=4] {'lag'}, use_global_device_ids=true, to_apply=%region_23.24 | all-reduce | flops 4096 | bytes 32768 | tf_op jit(solution)/shard_map/psum | solution.py:54
  626.6 31.3 %psum.152 = f32[1024]{0:T(1024)S(1)} all-reduce(f32[1024]{0:T(1024)S(1)} %multiply_reduce_fusion.13), channel_id=1, replica_groups=mesh['pair'=2,'day'=16,'lag'=4] {'day'}, use_global_device_ids=true, to_apply=%region_25.26 | all-reduce | flops 1024 | bytes 8192 | tf_op jit(solution)/shard_map/psum | solution.py:55
  658.1 9.3 multiply_reduce_fusion.3
  667.5 93.6 %all-reduce.8.cloned.1.call-done = f32[1024,512]{1,0:T(8,128)} async-done(((f32[1024,512]{1,0:T(8,128)}), f32[1024,512]{1,0:T(8,128)}) %all-reduce.8.cloned.1.call-update) | async-done | bytes 2097168 | tf_op jit(solution)/shard_map/psum | solution.py:57
  777.1 16.1 %psum.155 = f32[1024,4]{1,0:T(8,128)S(1)} all-reduce(f32[1024,4]{1,0:T(8,128)S(1)} %multiply_reduce_fusion.2), channel_id=1, replica_groups=mesh['pair'=2,'day'=16,'lag'=4] {'lag'}, use_global_device_ids=true, to_apply=%region_31.32 | all-reduce | flops 4096 | bytes 32768 | tf_op jit(solution)/shard_map/psum | solution.py:52
  800.4 16.1 %psum.156 = f32[1024,4]{1,0:T(8,128)S(1)} all-reduce(f32[1024,4]{1,0:T(8,128)S(1)} %multiply_reduce_fusion.1), channel_id=1, replica_groups=mesh['pair'=2,'day'=16,'lag'=4] {'lag'}, use_global_device_ids=true, to_apply=%region_33.34 | all-reduce | flops 4096 | bytes 32768 | tf_op jit(solution)/shard_map/psum | solution.py:54
  816.7 31.3 %psum.157 = f32[1024]{0:T(1024)S(1)} all-reduce(f32[1024]{0:T(1024)S(1)} %multiply_reduce_fusion.12), channel_id=1, replica_groups=mesh['pair'=2,'day'=16,'lag'=4] {'day'}, use_global_device_ids=true, to_apply=%region_35.36 | all-reduce | flops 1024 | bytes 8192 | tf_op jit(solution)/shard_map/psum | solution.py:55
  848.4 9.3 multiply_reduce_fusion
  857.8 28.7 %psum.159 = f32[1024]{0:T(1024)S(1)} all-reduce(f32[1024]{0:T(1024)S(1)} %get-tuple-element.11), channel_id=1, replica_groups=mesh['pair'=2,'day'=16,'lag'=4] {'day'}, use_global_device_ids=true, to_apply=%region_39.40 | all-reduce | flops 1024 | bytes 8192 | tf_op jit(solution)/shard_map/psum | solution.py:57
  887.6 63.8 %all-reduce.10.cloned.1.call-done = f32[1024,512]{1,0:T(8,128)} async-done(((f32[1024,512]{1,0:T(8,128)}), f32[1024,512]{1,0:T(8,128)}) %all-reduce.10.cloned.1.call-update) | async-done | bytes 2097168 | tf_op jit(solution)/shard_map/psum | solution.py:57
  (47 shorter events, 91.8 us)
Async XLA Ops:
  7.2 157.5 %all-gather.2.cloned.1.call-start = ((), (), s32[]{:S(2)}) async-start(), calls=%async_computation | async-start | bytes 20971520 | tf_op jit(solution)/shard_map/all_gather | solution.py:31
  7.9 371.1 %all-reduce.12.cloned.1.call-start = ((), (), s32[]{:S(2)}) async-start(), calls=%async_computation.4 | async-start | bytes 12582912 | tf_op jit(solution)/shard_map/psum | solution.py:42
  254.6 316.4 %all-reduce.6.cloned.1.call-start = ((), (), s32[]{:S(2)}) async-start(), calls=%async_computation.1 | async-start | bytes 4194304 | tf_op jit(solution)/shard_map/psum | solution.py:57
  477.5 283.6 %all-reduce.8.cloned.1.call-start = ((), (), s32[]{:S(2)}) async-start(), calls=%async_computation.2 | async-start | bytes 4194304 | tf_op jit(solution)/shard_map/psum | solution.py:57
  667.4 284.0 %all-reduce.10.cloned.1.call-start = ((), (), s32[]{:S(2)}) async-start(), calls=%async_computation.3 | async-start | bytes 4194304 | tf_op jit(solution)/shard_map/psum | solution.py:57
Sparse Core Ops, SparseCore 0:
  9.6 154.9 all-gather.1
  254.8 124.2 all-reduce.11
  477.6 93.3 all-reduce.5
  667.6 93.5 all-reduce.7
  857.9 93.5 all-reduce.9
where the time goes:
time: 972 us; the launch traced here: 961 us
  waiting for transfers between devices  492 us (51%)
  blocking collectives  255 us (26%)
  other arithmetic  142 us (15%)
  local copies, waits for them, and re-layouts  43.3 us (4%)
  matrix products  14.5 us (1%)
  between operations  14.2 us (1%)
    psum x3, waiting for transfers between devices, per_device(): lax.psum((jnp.sum(weight[:, :, None] * xn, axis=1), jnp.sum(weight, axis=...  251 us
    psum x1, waiting for transfers between devices, per_device(): lax.psum((jnp.sum(xn, axis=1), jnp.sum(cosine, axis=1), jnp.sum(sine, axi...  124 us
    all_gather x1, waiting for transfers between devices, per_device(): piece = lax.all_gather(corr, 'lag', axis=2, tiled=True)  116 us
    psum x3, blocking collectives, per_device(): rbar = lax.psum(jnp.sum(res, axis=1), 'day') / days  94 us
    psum x3, blocking collectives, per_device(): res = lax.psum(spread, 'lag') / lags  48.3 us
    psum x3, blocking collectives, per_device(): coh = lax.psum(inner, 'lag') / lags  48.2 us
    reduce_sum x1, other arithmetic, per_device(): jnp.sum(xn, axis=1)  32.9 us
    psum x1, blocking collectives, per_device(): lax.psum((jnp.sum(weight[:, :, None] * xn, axis=1), jnp.sum(weight, axis=...  28.7 us
  transfers between devices with their start and end apart: 5, of which 5 were waited for; matrix products, arithmetic and copies ran while one was open for 3% of the time, Pallas kernels for 0%

commit v1 on v0

v1 whole, which is shorter than its diff:
```python
import functools

import jax
import jax.numpy as jnp
import numpy as np
from jax import lax
from jax.experimental import pallas as pl
from jax.experimental.pallas import tpu as pltpu
from jax.sharding import PartitionSpec as P

ITERS = 3
EPS = 1e-06
HBM = pl.BlockSpec(memory_space=pl.ANY)
VMEM = pl.BlockSpec(memory_space=pltpu.VMEM)
F32 = jnp.float32


def hilbert_rows(rows, lags):
    offset = (np.arange(lags)[None, :] - np.arange(rows)[:, None]) % lags
    odd = offset % 2 == 1
    angle = np.pi * offset / lags
    value = np.where(odd, 2.0 / lags * np.cos(angle) / np.where(odd, np.sin(angle), 1.0), 0.0)
    return value.astype(np.float32).astype(jnp.bfloat16)


def peer(k, me_d, me_l):
    k = lax.rem(k * 37, 64)
    z = lax.rem(me_d // 4 + k // 16, 4)
    y = lax.rem(lax.rem(me_d, 4) + lax.rem(k // 4, 4), 4)
    x = lax.rem(me_l // 2 + lax.rem(k // 2, 2), 2)
    c = lax.rem(lax.rem(me_l, 2) + lax.rem(k, 2), 2)
    return z * 4 + y, x * 2 + c


def entry_barrier(d, l):
    barrier = pltpu.get_barrier_semaphore()

    def greet(k, carry):
        td, tl = peer(k, d, l)
        pl.semaphore_signal(barrier, inc=1, device_id={"day": td, "lag": tl})
        return carry

    lax.fori_loop(1, 64, greet, 0)
    pl.semaphore_wait(barrier, 63)


def exchange_kernel(rows, width, x_ref, o_ref, own_sem, send_sem, recv_sem):
    d = lax.axis_index("day")
    l = lax.axis_index("lag")
    entry_barrier(d, l)
    lanes = pl.ds(pl.multiple_of(l * width, width), width)

    def block(td, tl):
        return x_ref.at[pl.ds(pl.multiple_of((td * 4 + tl) * rows, rows), rows), :]

    def send(k, carry):
        td, tl = peer(k, d, l)
        pltpu.make_async_remote_copy(
            src_ref=block(td, tl),
            dst_ref=o_ref.at[d, :, lanes],
            send_sem=send_sem,
            recv_sem=recv_sem,
            device_id={"day": td, "lag": tl},
        ).start()
        return carry

    lax.fori_loop(1, 64, send, 0)
    own = pltpu.make_async_copy(block(d, l), o_ref.at[d, :, lanes], recv_sem)
    own.start()
    pltpu.make_async_copy(o_ref, o_ref, recv_sem).wait()
    most = x_ref.at[pl.ds(0, 63 * rows), :]
    pltpu.make_async_copy(most, most, send_sem).wait()


def exchange(x):
    total, width = x.shape
    rows = total // 64
    return pl.pallas_call(
        functools.partial(exchange_kernel, rows, width),
        out_shape=jax.ShapeDtypeStruct((16, rows, 4 * width), x.dtype),
        in_specs=[HBM],
        out_specs=HBM,
        scratch_shapes=[pltpu.SemaphoreType.DMA] * 3,
        compiler_params=pltpu.CompilerParams(collective_id=0, has_side_effects=True),
        name="exchange",
    )(x)


def group4(x):
    n = x.shape[0]
    row = lax.broadcasted_iota(jnp.int32, x.shape, 0)
    other = jnp.where(row % 2 == 0, pltpu.roll(x, n - 1, 0), pltpu.roll(x, 1, 0))
    x = x + other
    other = jnp.where(row % 4 < 2, pltpu.roll(x, n - 2, 0), pltpu.roll(x, 2, 0))
    return x + other


def stack_kernel(g_ref, x_ref, pws_ref, rob_ref, w_ref, k_ref, xn_ref, st_ref, cs_ref, ss_ref, rms_ref, coh_ref, wt_ref):
    ndev, rows, lags = x_ref.shape
    days = ndev * 4
    step = g_ref.shape[0]
    zero = jnp.zeros((rows, 128), F32)

    def lanes(x):
        return jnp.broadcast_to(jnp.sum(x, axis=1, keepdims=True), (rows, 128))

    def wide(x):
        return jnp.concatenate([x] * (lags // 128), axis=1)

    @pl.when(pl.program_id(0) == 0)
    def _():
        for i in range(lags // step):
            cut = i * step
            if cut:
                k_ref[cut:cut + step, :cut] = g_ref[:, lags - cut:]
            k_ref[cut:cut + step, cut:] = g_ref[:, :lags - cut]

    st_ref[...] = jnp.zeros((rows, lags), F32)

    @pl.loop(0, ndev)
    def _(d):
        data = x_ref[d].astype(F32)
        rms = jnp.sqrt(lanes(data * data) / lags + EPS)
        inv = 1.0 / rms
        rms_ref[d] = 10.0 * inv
        xn = data * wide(inv)
        xn_ref[d] = xn
        st_ref[...] += xn

    tile = 256

    @pl.loop(0, lags // tile)
    def _(t):
        at = pl.ds(pl.multiple_of(t * tile, tile), tile)
        quad = jnp.dot(x_ref[...].reshape(ndev * rows, lags), k_ref[:, at], preferred_element_type=F32)
        csum = jnp.zeros((rows, tile), F32)
        ssum = jnp.zeros((rows, tile), F32)
        for d in range(ndev):
            data = x_ref[d, :, at].astype(F32)
            q = quad[d * rows:(d + 1) * rows]
            top = rms_ref[d]
            inv = jnp.minimum(lax.rsqrt(data * data + q * q), jnp.concatenate([top, top], axis=1))
            csum = csum + data * inv
            ssum = ssum + q * inv
        csum = group4(csum)
        ssum = group4(ssum)
        lin = group4(st_ref[:, at])
        st_ref[:, at] = lin / days * ((csum * csum + ssum * ssum) / (days * days))

    pws_ref[...] = st_ref[...]
    for _ in range(ITERS):
        stack = st_ref[...]
        msq = lanes(stack * stack) / lags
        st_ref[...] = stack * wide(1.0 / jnp.sqrt(msq + EPS))

        def fit(d, rbar):
            coh = lanes(xn_ref[d] * st_ref[...]) / lags
            diff = xn_ref[d] - wide(coh) * st_ref[...]
            res = lanes(diff * diff) / lags
            coh_ref[d] = coh
            wt_ref[d] = res
            return rbar + res

        rbar = lax.fori_loop(0, ndev, fit, zero)
        rbar = group4(rbar) / days
        st_ref[...] = jnp.zeros((rows, lags), F32)

        def mix(d, total):
            weight = (0.1 + jnp.abs(coh_ref[d])) / (wt_ref[d] + rbar + EPS)
            wt_ref[d] = weight
            st_ref[...] += wide(weight) * xn_ref[d]
            return total + weight

        total = group4(lax.fori_loop(0, ndev, mix, zero))
        st_ref[...] = group4(st_ref[...])
    rob_ref[...] = st_ref[...] * wide(1.0 / total)
    lane = lax.broadcasted_iota(jnp.int32, (rows, 128), 1)
    w_ref[...] = lax.fori_loop(0, ndev, lambda d, w: jnp.where(lane == d, wt_ref[d] / total, w), zero)


def stacks(g, recv):
    ndev, rows, lags = recv.shape
    part = 16
    row = pl.BlockSpec((part, lags), lambda i: (i, 0))
    out = jax.ShapeDtypeStruct((rows, lags), F32)
    wide = pltpu.VMEM((part, lags), F32)
    thin = pltpu.VMEM((ndev, part, 128), F32)
    return pl.pallas_call(
        stack_kernel,
        out_shape=(out, out, jax.ShapeDtypeStruct((rows, 128), F32)),
        grid=(rows // part,),
        in_specs=[pl.BlockSpec(g.shape, lambda i: (0, 0)), pl.BlockSpec((ndev, part, lags), lambda i: (0, i, 0))],
        out_specs=(row, row, pl.BlockSpec((part, 128), lambda i: (i, 0))),
        scratch_shapes=[
            pltpu.VMEM((lags, lags), jnp.bfloat16),
            pltpu.VMEM((ndev, part, lags), F32),
            wide, wide, wide, thin, thin, thin,
        ],
        compiler_params=pltpu.CompilerParams(vmem_limit_bytes=48 * 2**20),
        name="stacks",
    )(g, recv)


def spread_kernel(rows, pws_ref, rob_ref, w_ref, pws_out, rob_out, w_out, send_sems, recv_sems):
    d = lax.axis_index("day")
    l = lax.axis_index("lag")
    entry_barrier(d, l)
    mine = d * 4 + l
    at = pl.ds(pl.multiple_of(mine * rows, rows), rows)

    def pairs(td, tl):
        yield pws_ref.at[tl], pws_out.at[at, :]
        yield rob_ref.at[tl], rob_out.at[at, :]
        yield w_ref.at[td], w_out.at[mine]

    def send(k, carry):
        td, tl = peer(k, d, l)
        for i, (src, dst) in enumerate(pairs(td, tl)):
            pltpu.make_async_remote_copy(
                src_ref=src, dst_ref=dst, send_sem=send_sems.at[i], recv_sem=recv_sems.at[i],
                device_id={"day": td, "lag": tl},
            ).start()
        return carry

    lax.fori_loop(1, 64, send, 0)
    for i, (src, dst) in enumerate(pairs(d, l)):
        pltpu.make_async_copy(src, dst, recv_sems.at[i]).start()
    for i, out in enumerate((pws_out, rob_out, w_out)):
        pltpu.make_async_copy(out, out, recv_sems.at[i]).wait()
    for i, most in enumerate((pws_out.at[pl.ds(0, 63 * rows)], rob_out.at[pl.ds(0, 63 * rows)], w_out.at[pl.ds(0, 63)])):
        pltpu.make_async_copy(most, most, send_sems.at[i]).wait()


def spread(pws, rob, w):
    _, rows, width = pws.shape
    out = jax.ShapeDtypeStruct((64 * rows, width), F32)
    return pl.pallas_call(
        functools.partial(spread_kernel, rows),
        out_shape=(out, out, jax.ShapeDtypeStruct((64,) + w.shape[1:], F32)),
        in_specs=[HBM] * 3,
        out_specs=(HBM,) * 3,
        scratch_shapes=[pltpu.SemaphoreType.DMA((3,)), pltpu.SemaphoreType.DMA((3,))],
        compiler_params=pltpu.CompilerParams(collective_id=1, has_side_effects=True),
        name="spread",
    )(pws, rob, w)


def per_device(corr):
    pairs, days_here, width = corr.shape
    lags = width * 4
    g = jnp.asarray(hilbert_rows(256, lags))
    recv = exchange(corr.reshape(pairs * days_here, width))
    pws, rob, w = stacks(g, recv)
    pws = pws[::4].reshape(16, 4, width).transpose(1, 0, 2)
    rob = rob[::4].reshape(16, 4, width).transpose(1, 0, 2)
    w = jnp.broadcast_to(w[:, :16].T.reshape(16, 1, 64), (16, 8, 64))
    w = jnp.concatenate([w, jnp.zeros_like(w)], axis=2)
    pws, rob, w = spread(pws, rob, w)
    return pws, rob, w[:, 0, :64].reshape(pairs, days_here)


def solution(mesh):
    return jax.shard_map(
        per_device,
        mesh=mesh,
        in_specs=(P("pair", "day", "lag"),),
        out_specs=(P("pair", "lag"), P("pair", "lag"), P("pair", "day")),
        check_vma=False,
    )
```

time: 972 us -> 223 us (0.23)
  waiting for transfers between devices: 492 us -> 0 us
  blocking collectives: 255 us -> 0 us
  Pallas kernels: 0 us -> 204 us
  other arithmetic: 142 us -> 0 us
  local copies, waits for them, and re-layouts: 43.3 us -> 15.2 us
  matrix products: 14.5 us -> 0 us
  between operations: 14.2 us -> 0.69 us
    psum x4 -> x0, waiting for transfers between devices: 375 us -> none  [the longest x3 251 us: per_device(): lax.psum((jnp.sum(weight[:, :, None] * xn, axis=1), jnp.sum(weight, axis=...]
    psum x14 -> x0, blocking collectives: 255 us -> none  [the longest x3 94 us: per_device(): rbar = lax.psum(jnp.sum(res, axis=1), 'day') / days]
    pallas_call x0 -> x3, Pallas kernels: none -> 204 us  [the longest x1 71.1 us: stacks(): pl.pallas_call(stack_kernel, out_shape=(out, out, jax.ShapeDtypeStruct((r...]
    all_gather x1 -> x0, waiting for transfers between devices: 116 us -> none  [per_device(): piece = lax.all_gather(corr, 'lag', axis=2, tiled=True)]
    reduce_sum x18 -> x0, other arithmetic: 113 us -> none  [the longest x1 32.9 us: per_device(): jnp.sum(xn, axis=1)]
    reshape x2 -> x1, local copies, waits for them, and re-layouts: 33.5 us -> 6.9 us  [per_device(): recv = exchange(corr.reshape(pairs * days_here, width))]
    dot_general x1 -> x0, other arithmetic: 19 us -> none  [per_device(): jnp.dot(piece.reshape(pairs * days_here, count), block, preferred_element...]
    dot_general x1 -> x0, matrix products: 14.5 us -> none  [per_device(): jnp.dot(piece.reshape(pairs * days_here, count), block, preferred_element...]
  transfers between devices with their start and end apart: 5 -> 0, of which waited for: 5 -> 0; matrix products, arithmetic and copies ran while one was open for 3% -> 0% of each run, Pallas kernels for 0% -> 0%
where the time goes in v1:
time: 223 us; the launch traced here: 220 us
  Pallas kernels  204 us (91%)
  local copies, waits for them, and re-layouts  15.2 us (7%)
    pallas_call x1, Pallas kernels, stacks(): pl.pallas_call(stack_kernel, out_shape=(out, out, jax.ShapeDtypeStruct((r...  71.1 us
    pallas_call x1, Pallas kernels, exchange(): pl.pallas_call(functools.partial(exchange_kernel, rows, width), out_shape...  68.1 us
    pallas_call x1, Pallas kernels, spread(): pl.pallas_call(functools.partial(spread_kernel, rows), out_shape=(out, ou...  65 us
    reshape x1, local copies, waits for them, and re-layouts, per_device(): recv = exchange(corr.reshape(pairs * days_here, width))  6.9 us
    unnamed x7, local copies, waits for them, and re-layouts  5.35 us

profile of v1, /device:TPU:1, one launch (start us, length us, event | category | flops | bytes accessed | tf_op | source)
XLA Modules:
  0.0 220.1 jit_solution(3841747882806441910)
XLA Ops:
  0.6 6.9 %reshape.17.x_ref = bf16[4096,512]{1,0:T(8,128)(2,1)} reshape(bf16[1024,4,512]{2,1,0:T(4,128)(2,1)} %param.2) | data formatting | bytes 8388608 | tf_op jit(solution)/shard_map/reshape | solution.py:252
  7.5 0.0 copy-start
  7.5 68.1 %exchange.1.x_ref = bf16[16,64,2048]{2,1,0:T(8,128)(2,1)} custom-call(bf16[4096,512]{1,0:T(8,128)(2,1)} %reshape.17.x_ref), custom_call_target="tpu_custom_call" | custom-call | tf_op jit(solution)/shard_map/exchange/pallas_call | solution.py:78
  75.7 0.0 copy-done
  75.7 71.1 %stacks.1 = (f32[64,2048]{1,0:T(8,128)S(1)}, f32[64,2048]{1,0:T(8,128)S(1)}, f32[64,128]{1,0:T(8,128)S(1)}) custom-call(bf16[256,2048]{1,0:T(8,128)(2,1)S(1)} %copy-done, bf16[16,64,2048]{2,1,0:T(8,128)(2,1)} %exchange.1.x_ref), custom_call_target="tpu_custom_call" | custom-call | tf_op jit(solution)/shard_map/stacks/pallas_call | solution.py:188
  146.8 0.1 slice.12
  146.9 0.1 copy.9
  147.0 0.7 concatenate.3.w_ref
  147.6 0.1 slice.13
  147.7 0.7 bitcast_bitcast_fusion
  148.4 65.0 %spread.1 = (f32[1024,512]{1,0:T(8,128)}, f32[1024,512]{1,0:T(8,128)}, f32[64,8,128]{2,1,0:T(8,128)}) custom-call(f32[4,16,512]{2,1,0:T(8,128)} %get-tuple-element.22.pws_ref, f32[4,16,512]{2,1,0:T(8,128)} %get-tuple-element.21.rob_ref, f32[16,8,128]{2,1,0:T(8,128)} %concatenate.3.w_ref), custom_call_target="tpu_custom_call" | custom-call | tf_op jit(solution)/shard_map/spread/pallas_call | solution.py:237
  213.4 1.0 slice_reduce_fusion
  214.4 0.3 reshape_squeeze.3
  214.7 0.8 copy.10
  215.5 0.0 copy-start.1
  215.5 3.2 %copy.17 = f32[1024,512]{1,0:T(8,128)} copy(f32[1024,512]{1,0:T(8,128)} %get-tuple-element.26) | data formatting | bytes 4194304
  218.7 0.0 copy-done.1
  218.7 1.3 copy.18
  (2 shorter events, 0.0 us)
Async XLA Ops:
  7.5 68.1 %copy-start = (bf16[256,2048]{1,0:T(8,128)(2,1)S(1)}, bf16[256,2048]{1,0:T(8,128)(2,1)}, u32[]{:S(2)}) copy-start(bf16[256,2048]{1,0:T(8,128)(2,1)} %constant.4.clone.g_ref) | copy-start | bytes 3145732
  215.5 3.2 %copy-start.1 = (f32[1024,512]{1,0:T(8,128)S(1)}, f32[1024,512]{1,0:T(8,128)}, u32[]{:S(2)}) copy-start(f32[1024,512]{1,0:T(8,128)} %get-tuple-element.27) | copy-start | bytes 6291460

commit v2 on v1

v2 whole, which is shorter than its diff:
```python
import functools

import jax
import jax.numpy as jnp
import numpy as np
from jax import lax
from jax.experimental import pallas as pl
from jax.experimental.pallas import tpu as pltpu
from jax.sharding import PartitionSpec as P

ITERS = 3
EPS = 1e-06
HBM = pl.BlockSpec(memory_space=pl.ANY)
VMEM = pl.BlockSpec(memory_space=pltpu.VMEM)
F32 = jnp.float32


def hilbert_rows(rows, lags):
    offset = (np.arange(lags)[None, :] - np.arange(rows)[:, None]) % lags
    odd = offset % 2 == 1
    angle = np.pi * offset / lags
    value = np.where(odd, 2.0 / lags * np.cos(angle) / np.where(odd, np.sin(angle), 1.0), 0.0)
    return value.astype(np.float32).astype(jnp.bfloat16)


def peer(k, me_d, me_l):
    a = lax.rem(k, 4)
    z = lax.rem(me_d // 4 + a, 4)
    y = lax.rem(lax.rem(me_d, 4) + a + k // 4, 4)
    x = lax.rem(me_l // 2 + a + k // 16, 2)
    c = lax.rem(me_l + k // 32, 2)
    return z * 4 + y, x * 2 + c


def entry_barrier(d, l):
    barrier = pltpu.get_barrier_semaphore()

    def greet(k, carry):
        td, tl = peer(k, d, l)
        pl.semaphore_signal(barrier, inc=1, device_id={"day": td, "lag": tl})
        return carry

    lax.fori_loop(1, 64, greet, 0)
    pl.semaphore_wait(barrier, 63)


def group4(x):
    n = x.shape[0]
    row = lax.broadcasted_iota(jnp.int32, x.shape, 0)
    other = jnp.where(row % 2 == 0, pltpu.roll(x, n - 1, 0), pltpu.roll(x, 1, 0))
    x = x + other
    other = jnp.where(row % 4 < 2, pltpu.roll(x, n - 2, 0), pltpu.roll(x, 2, 0))
    return x + other


def wide(x, lanes):
    return jnp.concatenate([x] * (lanes // 128), axis=1)


def fold(x):
    total = x[:, :128]
    for j in range(128, x.shape[1], 128):
        total = total + x[:, j:j + 128]
    return total


def lane_sum(ref):
    ndev, rows, lanes = ref.shape
    total = jnp.sum(ref[...].reshape(ndev * rows, lanes), axis=1, keepdims=True)
    return jnp.broadcast_to(total, (ndev * rows, lanes)).reshape(ndev, rows, lanes)


def day_sum(x):
    total = x[0]
    for d in range(1, x.shape[0]):
        total = total + x[d]
    return group4(total)


def stack_kernel(parts, g_ref, x_ref, pws_ref, rob_ref, w_ref,
                 recv, k_ref, xb_ref, x32_ref, st_ref, part_ref, inv_ref, coh_ref, wt_ref, send_sem, recv_sems):
    me_d = lax.axis_index("day")
    me_l = lax.axis_index("lag")
    ndev, quads, here, lags = recv.shape[1:]
    rows = quads * here
    days = ndev * here
    width = lags // 4
    entry_barrier(me_d, me_l)
    lanes = pl.ds(pl.multiple_of(me_l * width, width), width)

    def block(r, td, tl):
        return x_ref.at[pl.ds(((td * 4 + tl) * parts + r) * quads, quads)]

    for r in range(parts):
        def send(k, carry):
            td, tl = peer(k, me_d, me_l)
            pltpu.make_async_remote_copy(
                src_ref=block(r, td, tl),
                dst_ref=recv.at[r, me_d, :, :, lanes],
                send_sem=send_sem,
                recv_sem=recv_sems.at[r],
                device_id={"day": td, "lag": tl},
            ).start()
            return carry

        lax.fori_loop(1, 64, send, 0)
        pltpu.make_async_copy(block(r, me_d, me_l), recv.at[r, me_d, :, :, lanes], recv_sems.at[r]).start()

    step = g_ref.shape[0]
    for i in range(lags // step):
        cut = i * step
        if cut:
            k_ref[cut:cut + step, :cut] = g_ref[:, lags - cut:]
        k_ref[cut:cut + step, cut:] = g_ref[:, :lags - cut]

    def one_part(r, carry):
        pltpu.make_async_copy(recv.at[r], recv.at[r], recv_sems.at[r]).wait()

        @pl.loop(0, ndev, unroll=2)
        def _(d):
            x = recv[r, d].reshape(rows, lags)
            xb_ref[d] = x
            data = x.astype(F32)
            x32_ref[d] = data
            part_ref[d] = fold(data * data)

        inv_ref[...] = 1.0 / jnp.sqrt(lane_sum(part_ref) / lags + EPS)
        tile = 256

        @pl.loop(0, lags // tile, unroll=2)
        def _(t):
            at = pl.ds(pl.multiple_of(t * tile, tile), tile)
            quad = jnp.dot(xb_ref[...].reshape(ndev * rows, lags), k_ref[:, at], preferred_element_type=F32)
            lin = jnp.zeros((rows, tile), F32)
            csum = jnp.zeros((rows, tile), F32)
            ssum = jnp.zeros((rows, tile), F32)
            for d in range(ndev):
                data = x32_ref[d, :, at]
                q = quad[d * rows:(d + 1) * rows]
                scale = wide(inv_ref[d], tile)
                inv = jnp.minimum(lax.rsqrt(data * data + q * q), 10.0 * scale)
                lin = lin + data * scale
                csum = csum + data * inv
                ssum = ssum + q * inv
            csum = group4(csum)
            ssum = group4(ssum)
            st_ref[:, at] = group4(lin) / days * ((csum * csum + ssum * ssum) / (days * days))

        out = pl.ds(pl.multiple_of(r * rows, rows), rows)
        pws_ref[out, :] = st_ref[...]
        for step in range(ITERS):
            stack = st_ref[...]
            msq = jnp.sum(fold(stack * stack), axis=1, keepdims=True) / lags
            st_ref[...] = stack * (1.0 / jnp.sqrt(msq + EPS))

            @pl.loop(0, ndev, unroll=4)
            def _(d):
                part_ref[d] = fold(x32_ref[d] * st_ref[...])

            coh_ref[...] = lane_sum(part_ref) * inv_ref[...] / lags

            @pl.loop(0, ndev, unroll=4)
            def _(d):
                diff = x32_ref[d] * wide(inv_ref[d], lags) - wide(coh_ref[d], lags) * st_ref[...]
                part_ref[d] = fold(diff * diff)

            res = lane_sum(part_ref) / lags
            rbar = day_sum(res) / days
            weight = (0.1 + jnp.abs(coh_ref[...])) / (res + rbar + EPS)
            total = day_sum(weight)
            wt_ref[...] = weight * inv_ref[...]
            chunk = 512

            @pl.loop(0, lags // chunk)
            def _(t):
                at = pl.ds(pl.multiple_of(t * chunk, chunk), chunk)
                mix = wide(wt_ref[0], chunk) * x32_ref[0, :, at]
                for d in range(1, ndev):
                    mix = mix + wide(wt_ref[d], chunk) * x32_ref[d, :, at]
                st_ref[:, at] = group4(mix)

            if step == ITERS - 1:
                rob_ref[out, :] = st_ref[...] * wide(1.0 / total, lags)
                lane = lax.broadcasted_iota(jnp.int32, (rows, 128), 1)
                shares = jnp.zeros((rows, 128), F32)
                for d in range(ndev):
                    shares = jnp.where(lane == d, weight[d] / total, shares)
                w_ref[out, :] = shares
        return carry

    lax.fori_loop(0, parts, one_part, 0)
    for r in range(parts):
        most = x_ref.at[pl.ds(0, 63 * quads)]
        pltpu.make_async_copy(most, most, send_sem).wait()


def stacks(g, x):
    pairs, here, width = x.shape
    lags = 4 * width
    parts = 4
    quads = pairs // 64 // parts
    rows = pairs // 64 * here
    part = quads * here
    out = jax.ShapeDtypeStruct((rows, lags), F32)
    thin = pltpu.VMEM((16, part, 128), F32)
    return pl.pallas_call(
        functools.partial(stack_kernel, parts),
        out_shape=(out, out, jax.ShapeDtypeStruct((rows, 128), F32)),
        in_specs=[VMEM, HBM],
        out_specs=(VMEM,) * 3,
        scratch_shapes=[
            pltpu.VMEM((parts, 16, quads, here, lags), x.dtype),
            pltpu.VMEM((lags, lags), jnp.bfloat16),
            pltpu.VMEM((16, part, lags), jnp.bfloat16),
            pltpu.VMEM((16, part, lags), F32),
            pltpu.VMEM((part, lags), F32),
            thin, thin, thin, thin,
            pltpu.SemaphoreType.DMA,
            pltpu.SemaphoreType.DMA((parts,)),
        ],
        compiler_params=pltpu.CompilerParams(collective_id=0, has_side_effects=True, vmem_limit_bytes=50 * 2**20),
        name="stacks",
    )(g, x)


def spread_kernel(rows, pws_ref, rob_ref, w_ref, pws_out, rob_out, w_out, send_sems, recv_sems):
    d = lax.axis_index("day")
    l = lax.axis_index("lag")
    entry_barrier(d, l)
    mine = d * 4 + l
    at = pl.ds(pl.multiple_of(mine * rows, rows), rows)

    def pairs(td, tl):
        yield pws_ref.at[tl], pws_out.at[at, :]
        yield rob_ref.at[tl], rob_out.at[at, :]
        yield w_ref.at[td], w_out.at[mine]

    def send(k, carry):
        td, tl = peer(k, d, l)
        for i, (src, dst) in enumerate(pairs(td, tl)):
            pltpu.make_async_remote_copy(
                src_ref=src, dst_ref=dst, send_sem=send_sems.at[i], recv_sem=recv_sems.at[i],
                device_id={"day": td, "lag": tl},
            ).start()
        return carry

    lax.fori_loop(1, 64, send, 0)
    for i, (src, dst) in enumerate(pairs(d, l)):
        pltpu.make_async_copy(src, dst, recv_sems.at[i]).start()
    for i, out in enumerate((pws_out, rob_out, w_out)):
        pltpu.make_async_copy(out, out, recv_sems.at[i]).wait()
    for i, most in enumerate((pws_out.at[pl.ds(0, 63 * rows)], rob_out.at[pl.ds(0, 63 * rows)], w_out.at[pl.ds(0, 63)])):
        pltpu.make_async_copy(most, most, send_sems.at[i]).wait()


def spread(pws, rob, w):
    _, rows, width = pws.shape
    out = jax.ShapeDtypeStruct((64 * rows, width), F32)
    return pl.pallas_call(
        functools.partial(spread_kernel, rows),
        out_shape=(out, out, jax.ShapeDtypeStruct((64,) + w.shape[1:], F32)),
        in_specs=[HBM] * 3,
        out_specs=(HBM,) * 3,
        scratch_shapes=[pltpu.SemaphoreType.DMA((3,)), pltpu.SemaphoreType.DMA((3,))],
        compiler_params=pltpu.CompilerParams(collective_id=1, has_side_effects=True),
        name="spread",
    )(pws, rob, w)


def per_device(corr):
    pairs, days_here, width = corr.shape
    lags = width * 4
    g = jnp.asarray(hilbert_rows(256, lags))
    pws, rob, w = stacks(g, corr)
    pws = pws[::4].reshape(16, 4, width).transpose(1, 0, 2)
    rob = rob[::4].reshape(16, 4, width).transpose(1, 0, 2)
    w = jnp.broadcast_to(w[:, :16].T.reshape(16, 1, 64), (16, 8, 64))
    w = jnp.concatenate([w, jnp.zeros_like(w)], axis=2)
    pws, rob, w = spread(pws, rob, w)
    return pws, rob, w[:, 0, :64].reshape(pairs, days_here)


def solution(mesh):
    return jax.shard_map(
        per_device,
        mesh=mesh,
        in_specs=(P("pair", "day", "lag"),),
        out_specs=(P("pair", "lag"), P("pair", "lag"), P("pair", "day")),
        check_vma=False,
    )
```

time: 223 us -> 155 us (0.70); the launches traced: 220 us -> 155 us
  Pallas kernels: 204 us -> 144 us
  local copies, waits for them, and re-layouts: 15.2 us -> 9.51 us
    pallas_call x2 -> x1, Pallas kernels: 139 us -> 83.1 us  [stacks(): pl.pallas_call(functools.partial(stack_kernel, parts), out_shape=(out, ou...]
    reshape x1 -> x0, local copies, waits for them, and re-layouts: 6.9 us -> none  [per_device(): recv = exchange(corr.reshape(pairs * days_here, width))]
    pallas_call x1, Pallas kernels: 65 us -> 61.4 us  [spread(): pl.pallas_call(functools.partial(spread_kernel, rows), out_shape=(out, ou...]
where the time goes in v2:
time: 155 us
  Pallas kernels  144 us (93%)
  local copies, waits for them, and re-layouts  9.51 us (6%)
    pallas_call x1, Pallas kernels, stacks(): pl.pallas_call(functools.partial(stack_kernel, parts), out_shape=(out, ou...  83.1 us
    pallas_call x1, Pallas kernels, spread(): pl.pallas_call(functools.partial(spread_kernel, rows), out_shape=(out, ou...  61.4 us
    unnamed x7, local copies, waits for them, and re-layouts  6.57 us

profile of v2, /device:TPU:1, one launch (start us, length us, event | category | flops | bytes accessed | tf_op | source)
XLA Modules:
  0.0 154.6 jit_solution(5305436532881070524)
XLA Ops:
  0.6 0.0 copy-start
  0.6 1.2 copy-done
  1.9 83.1 %stacks.1 = (f32[64,2048]{1,0:T(8,128)S(1)}, f32[64,2048]{1,0:T(8,128)S(1)}, f32[64,128]{1,0:T(8,128)S(1)}) custom-call(bf16[256,2048]{1,0:T(8,128)(2,1)S(1)} %copy-done, bf16[1024,4,512]{2,1,0:T(4,128)(2,1)} %x_ref.1), custom_call_target="tpu_custom_call" | custom-call | tf_op jit(solution)/shard_map/stacks/pallas_call | solution.py:206
  84.9 0.1 slice.12
  85.0 0.1 copy.9
  85.1 0.7 concatenate.3.w_ref
  85.8 0.1 slice.13
  85.9 0.7 bitcast_bitcast_fusion
  86.6 61.4 %spread.1 = (f32[1024,512]{1,0:T(8,128)}, f32[1024,512]{1,0:T(8,128)}, f32[64,8,128]{2,1,0:T(8,128)}) custom-call(f32[4,16,512]{2,1,0:T(8,128)} %get-tuple-element.22.pws_ref, f32[4,16,512]{2,1,0:T(8,128)} %get-tuple-element.21.rob_ref, f32[16,8,128]{2,1,0:T(8,128)} %concatenate.3.w_ref), custom_call_target="tpu_custom_call" | custom-call | tf_op jit(solution)/shard_map/spread/pallas_call | solution.py:259
  148.0 1.0 slice_reduce_fusion
  149.0 0.3 reshape_squeeze.3
  149.3 0.8 copy.10
  150.1 0.0 copy-start.1
  150.1 3.2 %copy.17 = f32[1024,512]{1,0:T(8,128)} copy(f32[1024,512]{1,0:T(8,128)} %get-tuple-element.26) | data formatting | bytes 4194304
  153.3 0.0 copy-done.1
  153.3 1.3 copy.18
  (2 shorter events, 0.0 us)
Async XLA Ops:
  0.6 1.2 copy-start
  150.1 3.2 %copy-start.1 = (f32[1024,512]{1,0:T(8,128)S(1)}, f32[1024,512]{1,0:T(8,128)}, u32[]{:S(2)}) copy-start(f32[1024,512]{1,0:T(8,128)} %get-tuple-element.27) | copy-start | bytes 6291460

commit v3 on v2

--- a/solution.py
+++ b/solution.py
@@ -78,7 +78,8 @@
 
 
 def stack_kernel(parts, g_ref, x_ref, pws_ref, rob_ref, w_ref,
-                 recv, k_ref, xb_ref, x32_ref, st_ref, part_ref, inv_ref, coh_ref, wt_ref, send_sem, recv_sems):
+                 recv, k_ref, xb_ref, x32_ref, st_ref, part_ref, inv_ref, coh_ref, wt_ref, share_ref,
+                 send_sem, recv_sems):
     me_d = lax.axis_index("day")
     me_l = lax.axis_index("lag")
     ndev, quads, here, lags = recv.shape[1:]
@@ -185,10 +186,21 @@
                 shares = jnp.zeros((rows, 128), F32)
                 for d in range(ndev):
                     shares = jnp.where(lane == d, weight[d] / total, shares)
-                w_ref[out, :] = shares
+                share_ref[out, :] = shares
         return carry
 
     lax.fori_loop(0, parts, one_part, 0)
+    units = []
+    for ref in (pws_ref, rob_ref):
+        top = jnp.max(jnp.abs(ref[...]), axis=(0, 1), keepdims=True)
+        top = jnp.maximum(top, 1e-30)
+        ref[...] = ref[...] * (16384.0 / top)
+        units.append(jnp.broadcast_to(top / 16384.0, (1, 128)))
+    shares = share_ref[...].T
+    lane = lax.broadcasted_iota(jnp.int32, (1, 128), 1)
+    for d in range(ndev):
+        row = jnp.where(lane == 64, units[0], shares[d:d + 1])
+        w_ref[d] = jnp.where(lane == 65, units[1], row)
     for r in range(parts):
         most = x_ref.at[pl.ds(0, 63 * quads)]
         pltpu.make_async_copy(most, most, send_sem).wait()
@@ -205,7 +217,7 @@
     thin = pltpu.VMEM((16, part, 128), F32)
     return pl.pallas_call(
         functools.partial(stack_kernel, parts),
-        out_shape=(out, out, jax.ShapeDtypeStruct((rows, 128), F32)),
+        out_shape=(out, out, jax.ShapeDtypeStruct((16, 1, 128), F32)),
         in_specs=[VMEM, HBM],
         out_specs=(VMEM,) * 3,
         scratch_shapes=[
@@ -215,6 +227,7 @@
             pltpu.VMEM((16, part, lags), F32),
             pltpu.VMEM((part, lags), F32),
             thin, thin, thin, thin,
+            pltpu.VMEM((128, 128), F32),
             pltpu.SemaphoreType.DMA,
             pltpu.SemaphoreType.DMA((parts,)),
         ],
@@ -223,48 +236,106 @@
     )(g, x)
 
 
-def spread_kernel(rows, pws_ref, rob_ref, w_ref, pws_out, rob_out, w_out, send_sems, recv_sems):
+def spread_kernel(rows, pws_ref, rob_ref, w_ref, pws_out, rob_out, w_out, w0, w1, send_sems, lag_sems, ring_sems, last_sems):
     d = lax.axis_index("day")
     l = lax.axis_index("lag")
-    entry_barrier(d, l)
-    mine = d * 4 + l
-    at = pl.ds(pl.multiple_of(mine * rows, rows), rows)
-
-    def pairs(td, tl):
-        yield pws_ref.at[tl], pws_out.at[at, :]
-        yield rob_ref.at[tl], rob_out.at[at, :]
-        yield w_ref.at[td], w_out.at[mine]
-
-    def send(k, carry):
-        td, tl = peer(k, d, l)
-        for i, (src, dst) in enumerate(pairs(td, tl)):
-            pltpu.make_async_remote_copy(
-                src_ref=src, dst_ref=dst, send_sem=send_sems.at[i], recv_sem=recv_sems.at[i],
-                device_id={"day": td, "lag": tl},
-            ).start()
-        return carry
-
-    lax.fori_loop(1, 64, send, 0)
-    for i, (src, dst) in enumerate(pairs(d, l)):
-        pltpu.make_async_copy(src, dst, recv_sems.at[i]).start()
-    for i, out in enumerate((pws_out, rob_out, w_out)):
-        pltpu.make_async_copy(out, out, recv_sems.at[i]).wait()
-    for i, most in enumerate((pws_out.at[pl.ds(0, 63 * rows)], rob_out.at[pl.ds(0, 63 * rows)], w_out.at[pl.ds(0, 63)])):
+    z, y = d // 4, lax.rem(d, 4)
+    lag_peers = [{"day": d, "lag": lax.rem(l + k, 4)} for k in (1, 2, 3)]
+    z_of = [lax.rem(z + k, 4) for k in range(4)]
+    y_of = [lax.rem(y + k, 4) for k in range(4)]
+    z_peers = [{"day": z_of[k] * 4 + y, "lag": l} for k in (1, 3, 2)]
+    y_peers = [{"day": z * 4 + y_of[k], "lag": l} for k in (1, 3, 2)]
+    barrier = pltpu.get_barrier_semaphore()
+    for peer_id in lag_peers + z_peers + y_peers:
+        pl.semaphore_signal(barrier, inc=1, device_id=peer_id)
+    pl.semaphore_wait(barrier, 9)
+
+    def push(i, src, dst, sem, to):
+        pltpu.make_async_remote_copy(
+            src_ref=src, dst_ref=dst, send_sem=send_sems.at[i], recv_sem=sem, device_id=to
+        ).start()
+
+    def day_rows(day):
+        return pl.ds(pl.multiple_of(day * 4 * rows, 4 * rows), 4 * rows)
+
+    mine = pl.ds(pl.multiple_of((d * 4 + l) * rows, rows), rows)
+    srcs, outs = (pws_ref, rob_ref), (pws_out, rob_out)
+    for i in range(2):
+        for to in lag_peers:
+            push(i, srcs[i].at[to["lag"]], outs[i].at[mine], lag_sems.at[i], to)
+        pltpu.make_async_copy(srcs[i].at[l], outs[i].at[mine], lag_sems.at[i]).start()
+    for to in lag_peers:
+        push(2, w_ref, w0.at[l], lag_sems.at[2], to)
+    pltpu.make_async_copy(w_ref, w0.at[l], lag_sems.at[2]).start()
+
+    first, second = (z_peers, y_peers), (y_peers, z_peers)
+    for i in range(2):
+        block = outs[i].at[day_rows(d)]
+        pltpu.make_async_copy(block, block, lag_sems.at[i]).wait()
+        for n, to in enumerate(first[i]):
+            push(i, block, block, ring_sems.at[i, n], to)
+        for to in second[i]:
+            push(i, block, block, last_sems.at[i], to)
+    pltpu.make_async_copy(w0, w0, lag_sems.at[2]).wait()
+    for n, k in enumerate((1, 3, 2)):
+        push(2, w0.at[:, pl.ds(z_of[k] * 4, 4)], w1.at[z], ring_sems.at[2, n], z_peers[n])
+    for n, k in enumerate((1, 3, 2)):
+        push(2, w0.at[:, z * 4 + y_of[k]], w_out.at[d], last_sems.at[2], y_peers[n])
+    pltpu.make_async_copy(w0.at[:, d], w_out.at[d], last_sems.at[2]).start()
+    for n, k in enumerate((3, 1, 2)):
+        for i in range(2):
+            block = outs[i].at[day_rows((z_of[k] * 4 + y, z * 4 + y_of[k])[i])]
+            pltpu.make_async_copy(block, block, ring_sems.at[i, n]).wait()
+            for to in second[i]:
+                push(i, block, block, last_sems.at[i], to)
+        part = w1.at[z_of[k]]
+        pltpu.make_async_copy(part, part, ring_sems.at[2, n]).wait()
+        for m, j in enumerate((1, 3, 2)):
+            push(2, w1.at[z_of[k], :, y_of[j]], w_out.at[z_of[k] * 4 + y], last_sems.at[2], y_peers[m])
+        pltpu.make_async_copy(w1.at[z_of[k], :, y], w_out.at[z_of[k] * 4 + y], last_sems.at[2]).start()
+    for i in range(2):
+        most = outs[i].at[pl.ds(0, 48 * rows)]
+        pltpu.make_async_copy(most, most, last_sems.at[i]).wait()
+        most = outs[i].at[pl.ds(0, 63 * rows)]
         pltpu.make_async_copy(most, most, send_sems.at[i]).wait()
+    pltpu.make_async_copy(w_out, w_out, last_sems.at[2]).wait()
+    for part in (w_out, w_out, w_out.at[pl.ds(0, 4)]):
+        pltpu.make_async_copy(part, part, send_sems.at[2]).wait()
 
 
 def spread(pws, rob, w):
     _, rows, width = pws.shape
-    out = jax.ShapeDtypeStruct((64 * rows, width), F32)
+    out = jax.ShapeDtypeStruct((64 * rows, width), pws.dtype)
     return pl.pallas_call(
         functools.partial(spread_kernel, rows),
-        out_shape=(out, out, jax.ShapeDtypeStruct((64,) + w.shape[1:], F32)),
+        out_shape=(out, out, jax.ShapeDtypeStruct((16, 4, 1, 128), F32)),
         in_specs=[HBM] * 3,
         out_specs=(HBM,) * 3,
-        scratch_shapes=[pltpu.SemaphoreType.DMA((3,)), pltpu.SemaphoreType.DMA((3,))],
+        scratch_shapes=[
+            pltpu.VMEM((4, 16, 1, 128), F32),
+            pltpu.VMEM((4, 4, 4, 1, 128), F32),
+            pltpu.SemaphoreType.DMA((3,)),
+            pltpu.SemaphoreType.DMA((3,)),
+            pltpu.SemaphoreType.DMA((3, 3)),
+            pltpu.SemaphoreType.DMA((3,)),
+        ],
         compiler_params=pltpu.CompilerParams(collective_id=1, has_side_effects=True),
         name="spread",
     )(pws, rob, w)
+
+
+def encode(x):
+    power = x * x
+    power = power * power
+    power = power * power
+    return jnp.where(x < 0, -power, power).astype(jnp.bfloat16)
+
+
+def decode(code):
+    power = code.astype(F32)
+    fourth = lax.rsqrt(lax.rsqrt(jnp.maximum(jnp.abs(power), 2e-38)))
+    root = fourth * lax.rsqrt(fourth)
+    return jnp.where(power < 0, -root, root)
 
 
 def per_device(corr):
@@ -272,12 +343,13 @@
     lags = width * 4
     g = jnp.asarray(hilbert_rows(256, lags))
     pws, rob, w = stacks(g, corr)
-    pws = pws[::4].reshape(16, 4, width).transpose(1, 0, 2)
-    rob = rob[::4].reshape(16, 4, width).transpose(1, 0, 2)
-    w = jnp.broadcast_to(w[:, :16].T.reshape(16, 1, 64), (16, 8, 64))
-    w = jnp.concatenate([w, jnp.zeros_like(w)], axis=2)
+    pws = encode(pws[::4].reshape(16, 4, width).transpose(1, 0, 2))
+    rob = encode(rob[::4].reshape(16, 4, width).transpose(1, 0, 2))
     pws, rob, w = spread(pws, rob, w)
-    return pws, rob, w[:, 0, :64].reshape(pairs, days_here)
+    w = w.reshape(64, 128)
+    pws = decode(pws).reshape(64, 16, width) * w[:, 64].reshape(64, 1, 1)
+    rob = decode(rob).reshape(64, 16, width) * w[:, 65].reshape(64, 1, 1)
+    return pws.reshape(pairs, width), rob.reshape(pairs, width), w[:, :64].reshape(pairs, days_here)
 
 
 def solution(mesh):

time: 155 us -> 116 us (0.75)
  Pallas kernels: 144 us -> 103 us
  other arithmetic: 0 us -> 5.69 us
  local copies, waits for them, and re-layouts: 9.51 us -> 5.17 us
    pallas_call x1, Pallas kernels: 61.4 us -> 20.2 us  [spread(): pl.pallas_call(functools.partial(spread_kernel, rows), out_shape=(out, ou...]
    mul x0 -> x3, other arithmetic: none -> 4.34 us  [the longest x1 4.31 us: per_device(): pws = decode(pws).reshape(64, 16, width) * w[:, 64].reshape(64, 1, 1)]
    unnamed x7 -> x5, local copies, waits for them, and re-layouts: 6.57 us -> 2.61 us
where the time goes in v3:
time: 116 us; the launch traced here: 115 us
  Pallas kernels  103 us (89%)
  other arithmetic  5.69 us (5%)
  local copies, waits for them, and re-layouts  5.17 us (4%)
    pallas_call x1, Pallas kernels, stacks(): pl.pallas_call(functools.partial(stack_kernel, parts), out_shape=(out, ou...  83.3 us
    pallas_call x1, Pallas kernels, spread(): pl.pallas_call(functools.partial(spread_kernel, rows), out_shape=(out, ou...  20.2 us
    mul x1, other arithmetic, per_device(): pws = decode(pws).reshape(64, 16, width) * w[:, 64].reshape(64, 1, 1)  4.31 us
    unnamed x5, local copies, waits for them, and re-layouts  2.61 us

profile of v3, /device:TPU:1, one launch (start us, length us, event | category | flops | bytes accessed | tf_op | source)
XLA Modules:
  0.0 115.0 jit_solution(4783785819279752491)
XLA Ops:
  0.6 0.0 copy-start
  0.6 1.2 %copy-done = bf16[256,2048]{1,0:T(8,128)(2,1)S(1)} copy-done((bf16[256,2048]{1,0:T(8,128)(2,1)S(1)}, bf16[256,2048]{1,0:T(8,128)(2,1)}, u32[]{:S(2)}) %copy-start) | copy-done | bytes 1048600
  1.9 83.3 %stacks.1 = (f32[64,2048]{1,0:T(8,128)S(1)}, f32[64,2048]{1,0:T(8,128)S(1)}, f32[16,1,128]{2,1,0:T(1,128)S(1)}) custom-call(bf16[256,2048]{1,0:T(8,128)(2,1)S(1)} %copy-done, bf16[1024,4,512]{2,1,0:T(4,128)(2,1)} %x_ref.1), custom_call_target="tpu_custom_call" | custom-call | tf_op jit(solution)/shard_map/stacks/pallas_call | solution.py:218
  85.2 0.0 copy-start.1
  85.2 0.6 copy-done.1
  85.8 0.1 slice.15
  85.9 0.7 fusion.8.pws_ref
  86.6 0.1 slice.16
  86.7 0.7 fusion.9.rob_ref
  87.4 20.2 %spread.1 = (bf16[1024,512]{1,0:T(8,128)(2,1)}, bf16[1024,512]{1,0:T(8,128)(2,1)}, f32[16,4,1,128]{3,2,1,0:T(1,128)}) custom-call(bf16[4,16,512]{2,1,0:T(8,128)(2,1)} %fusion.8.pws_ref, bf16[4,16,512]{2,1,0:T(8,128)(2,1)} %fusion.9.rob_ref, f32[16,1,128]{2,1,0:T(1,128)} %copy-done.1), custom_call_target="tpu_custom_call" | custom-call | tf_op jit(solution)/shard_map/spread/pallas_call | solution.py:309
  107.5 1.0 slice_reduce_fusion
  108.6 0.1 mul.92
  108.6 0.1 mul.93
  108.7 0.1 mul.86
  108.8 0.1 mul.87
  108.9 1.1 reshape.33
  109.9 0.8 copy.16
  110.7 4.3 %fusion.6 = (f32[1024,512]{1,0:T(8,128)}, f32[1024,512]{1,0:T(8,128)}) fusion(bf16[1024,512]{1,0:T(8,128)(2,1)} %get-tuple-element.12, f32[1024]{0:T(1024)S(1)} %mul.87, f32[1024]{0:T(1024)S(1)} %mul.93, bf16[1024,512]{1,0:T(8,128)(2,1)} %get-tuple-element.14), kind=kLoop, calls=%fused_computation.14 | loop fusion | flops 8388608 | bytes 6299648 | tf_op jit(solution)/shard_map/mul | solution.py:350
  (4 shorter events, 0.1 us)
Async XLA Ops:
  0.6 1.2 %copy-start = (bf16[256,2048]{1,0:T(8,128)(2,1)S(1)}, bf16[256,2048]{1,0:T(8,128)(2,1)}, u32[]{:S(2)}) copy-start(bf16[256,2048]{1,0:T(8,128)(2,1)} %constant.2.clone.g_ref) | copy-start | bytes 3145732
  85.2 0.6 copy-start.1

commit v4 on v3

--- a/solution.py
+++ b/solution.py
@@ -25,8 +25,8 @@
 
 def peer(k, me_d, me_l):
     a = lax.rem(k, 4)
-    z = lax.rem(me_d // 4 + a, 4)
-    y = lax.rem(lax.rem(me_d, 4) + a + k // 4, 4)
+    z = lax.rem(me_d // 4 + a + k // 4, 4)
+    y = lax.rem(lax.rem(me_d, 4) + a, 4)
     x = lax.rem(me_l // 2 + a + k // 16, 2)
     c = lax.rem(me_l + k // 32, 2)
     return z * 4 + y, x * 2 + c

time: 116 us -> 102 us (0.88)
  Pallas kernels: 103 us -> 88.4 us
    pallas_call x1, Pallas kernels: 83.3 us -> 66.4 us  [stacks(): pl.pallas_call(functools.partial(stack_kernel, parts), out_shape=(out, ou...]
    pallas_call x1, Pallas kernels: 20.2 us -> 22 us  [spread(): pl.pallas_call(functools.partial(spread_kernel, rows), out_shape=(out, ou...]
where the time goes in v4:
time: 102 us; the launch traced here: 99.9 us
  Pallas kernels  88.4 us (87%)
  other arithmetic  5.69 us (6%)
  local copies, waits for them, and re-layouts  5.17 us (5%)
    pallas_call x1, Pallas kernels, stacks(): pl.pallas_call(functools.partial(stack_kernel, parts), out_shape=(out, ou...  66.4 us
    pallas_call x1, Pallas kernels, spread(): pl.pallas_call(functools.partial(spread_kernel, rows), out_shape=(out, ou...  22 us
    mul x1, other arithmetic, per_device(): pws = decode(pws).reshape(64, 16, width) * w[:, 64].reshape(64, 1, 1)  4.31 us
    unnamed x5, local copies, waits for them, and re-layouts  2.61 us

profile of v4, /device:TPU:1, one launch (start us, length us, event | category | flops | bytes accessed | tf_op | source)
XLA Modules:
  0.0 99.9 jit_solution(1093426370040463560)
XLA Ops:
  0.6 0.0 copy-start
  0.6 1.2 %copy-done = bf16[256,2048]{1,0:T(8,128)(2,1)S(1)} copy-done((bf16[256,2048]{1,0:T(8,128)(2,1)S(1)}, bf16[256,2048]{1,0:T(8,128)(2,1)}, u32[]{:S(2)}) %copy-start) | copy-done | bytes 1048600
  1.9 66.4 %stacks.1 = (f32[64,2048]{1,0:T(8,128)S(1)}, f32[64,2048]{1,0:T(8,128)S(1)}, f32[16,1,128]{2,1,0:T(1,128)S(1)}) custom-call(bf16[256,2048]{1,0:T(8,128)(2,1)S(1)} %copy-done, bf16[1024,4,512]{2,1,0:T(4,128)(2,1)} %x_ref.1), custom_call_target="tpu_custom_call" | custom-call | tf_op jit(solution)/shard_map/stacks/pallas_call | solution.py:218
  68.3 0.0 copy-start.1
  68.3 0.6 copy-done.1
  68.9 0.1 slice.15
  69.0 0.7 fusion.8.pws_ref
  69.7 0.1 slice.16
  69.8 0.7 fusion.9.rob_ref
  70.5 22.0 %spread.1 = (bf16[1024,512]{1,0:T(8,128)(2,1)}, bf16[1024,512]{1,0:T(8,128)(2,1)}, f32[16,4,1,128]{3,2,1,0:T(1,128)}) custom-call(bf16[4,16,512]{2,1,0:T(8,128)(2,1)} %fusion.8.pws_ref, bf16[4,16,512]{2,1,0:T(8,128)(2,1)} %fusion.9.rob_ref, f32[16,1,128]{2,1,0:T(1,128)} %copy-done.1), custom_call_target="tpu_custom_call" | custom-call | tf_op jit(solution)/shard_map/spread/pallas_call | solution.py:309
  92.4 1.0 %slice_reduce_fusion = (f32[64]{0:T(128)S(1)}, f32[64]{0:T(128)S(1)}) fusion(f32[64,128]{1,0:T(8,128)} %bitcast.40), kind=kLoop, calls=%fused_computation.28 | loop fusion | bytes 1024 | tf_op jit(solution)/shard_map/slice | solution.py:351
  93.5 0.1 mul.92
  93.5 0.1 mul.93
  93.6 0.1 mul.86
  93.7 0.1 mul.87
  93.8 1.1 %reshape.33 = f32[1024,4]{1,0:T(8,128)S(1)} reshape(f32[64,64]{1,0:T(8,128)} %bitcast.41) | data formatting | bytes 32768 | tf_op jit(solution)/shard_map/reshape | solution.py:352
  94.8 0.8 copy.16
  95.6 4.3 %fusion.6 = (f32[1024,512]{1,0:T(8,128)}, f32[1024,512]{1,0:T(8,128)}) fusion(bf16[1024,512]{1,0:T(8,128)(2,1)} %get-tuple-element.12, f32[1024]{0:T(1024)S(1)} %mul.87, f32[1024]{0:T(1024)S(1)} %mul.93, bf16[1024,512]{1,0:T(8,128)(2,1)} %get-tuple-element.14), kind=kLoop, calls=%fused_computation.14 | loop fusion | flops 8388608 | bytes 6299648 | tf_op jit(solution)/shard_map/mul | solution.py:350
  (4 shorter events, 0.1 us)
Async XLA Ops:
  0.6 1.2 %copy-start = (bf16[256,2048]{1,0:T(8,128)(2,1)S(1)}, bf16[256,2048]{1,0:T(8,128)(2,1)}, u32[]{:S(2)}) copy-start(bf16[256,2048]{1,0:T(8,128)(2,1)} %constant.2.clone.g_ref) | copy-start | bytes 3145732
  68.3 0.6 copy-start.1

commit v5 on v2

--- a/solution.py
+++ b/solution.py
@@ -25,8 +25,8 @@
 
 def peer(k, me_d, me_l):
     a = lax.rem(k, 4)
-    z = lax.rem(me_d // 4 + a, 4)
-    y = lax.rem(lax.rem(me_d, 4) + a + k // 4, 4)
+    z = lax.rem(me_d // 4 + a + k // 4, 4)
+    y = lax.rem(lax.rem(me_d, 4) + a, 4)
     x = lax.rem(me_l // 2 + a + k // 16, 2)
     c = lax.rem(me_l + k // 32, 2)
     return z * 4 + y, x * 2 + c
@@ -77,14 +77,33 @@
     return group4(total)
 
 
-def stack_kernel(parts, g_ref, x_ref, pws_ref, rob_ref, w_ref,
-                 recv, k_ref, xb_ref, x32_ref, st_ref, part_ref, inv_ref, coh_ref, wt_ref, send_sem, recv_sems):
+def encode(x):
+    power = x * x
+    power = power * power
+    power = power * power
+    return jnp.where(x < 0, -power, power).astype(jnp.bfloat16)
+
+
+def decode(code):
+    power = code.astype(F32)
+    fourth = lax.rsqrt(lax.rsqrt(jnp.maximum(jnp.abs(power), 2e-38)))
+    root = fourth * lax.rsqrt(fourth)
+    return jnp.where(power < 0, -root, root)
+
+
+def stack_kernel(parts, g_ref, x_ref, pws_out, rob_out, tail_out,
+                 recv, gv_ref, k_ref, xb_ref, x32_ref, st_ref, part_ref, inv_ref, coh_ref, wt_ref, share_ref, unit_ref,
+                 pws_code, rob_code, tail_code,
+                 g_sem, send_sem, recv_sems, out_sems, lag_sems, ring_sems, last_sems, tail_sems):
     me_d = lax.axis_index("day")
     me_l = lax.axis_index("lag")
     ndev, quads, here, lags = recv.shape[1:]
     rows = quads * here
     days = ndev * here
     width = lags // 4
+    early = parts - 1
+    fetch = pltpu.make_async_copy(g_ref, gv_ref, g_sem)
+    fetch.start()
     entry_barrier(me_d, me_l)
     lanes = pl.ds(pl.multiple_of(me_l * width, width), width)
 
@@ -106,14 +125,67 @@
         lax.fori_loop(1, 64, send, 0)
         pltpu.make_async_copy(block(r, me_d, me_l), recv.at[r, me_d, :, :, lanes], recv_sems.at[r]).start()
 
+    fetch.wait()
     step = g_ref.shape[0]
     for i in range(lags // step):
         cut = i * step
         if cut:
-            k_ref[cut:cut + step, :cut] = g_ref[:, lags - cut:]
-        k_ref[cut:cut + step, cut:] = g_ref[:, :lags - cut]
-
-    def one_part(r, carry):
+            k_ref[cut:cut + step, :cut] = gv_ref[:, lags - cut:]
+        k_ref[cut:cut + step, cut:] = gv_ref[:, :lags - cut]
+
+    z, y = me_d // 4, lax.rem(me_d, 4)
+    z_of = [lax.rem(z + k, 4) for k in range(4)]
+    y_of = [lax.rem(y + k, 4) for k in range(4)]
+    lag_peers = [lax.rem(me_l + k, 4) for k in (1, 2, 3)]
+    z_peers = [{"day": z_of[k] * 4 + y, "lag": me_l} for k in (1, 3, 2)]
+    y_peers = [{"day": z * 4 + y_of[k], "lag": me_l} for k in (1, 3, 2)]
+    first, second = (z_peers, y_peers, z_peers), (y_peers, z_peers, y_peers)
+    codes, outs = (pws_code, rob_code, pws_code), (pws_out, rob_out, pws_out)
+    spans = (pl.ds(0, early), pl.ds(0, early), pl.ds(early, 1))
+
+    def push(i, src, dst, sem, to):
+        pltpu.make_async_remote_copy(
+            src_ref=src, dst_ref=dst, send_sem=out_sems.at[i], recv_sem=sem, device_id=to
+        ).start()
+
+    def to_lag_group(i):
+        dst = outs[i].at[spans[i], me_d, me_l]
+        for tl in lag_peers:
+            push(i, codes[i].at[spans[i], tl], dst, lag_sems.at[i], {"day": me_d, "lag": tl})
+        pltpu.make_async_copy(codes[i].at[spans[i], me_l], dst, lag_sems.at[i]).start()
+
+    def to_rings(i):
+        own = outs[i].at[spans[i], me_d]
+        pltpu.make_async_copy(own, own, lag_sems.at[i]).wait()
+        for n, to in enumerate(first[i]):
+            push(i, own, own, ring_sems.at[i, n], to)
+        for to in second[i]:
+            push(i, own, own, last_sems.at[i], to)
+
+    def forward(i):
+        for n, k in enumerate((3, 1, 2)):
+            day = (z_of[k] * 4 + y, z * 4 + y_of[k], z_of[k] * 4 + y)[i]
+            got = outs[i].at[spans[i], day]
+            pltpu.make_async_copy(got, got, ring_sems.at[i, n]).wait()
+            for to in second[i]:
+                push(i, got, got, last_sems.at[i], to)
+
+    def finish(i):
+        most = outs[i].at[spans[i], pl.ds(0, 12)]
+        pltpu.make_async_copy(most, most, last_sems.at[i]).wait()
+        for part in (outs[i].at[spans[i], pl.ds(0, 15)], codes[i].at[spans[i], pl.ds(0, 3)]):
+            pltpu.make_async_copy(part, part, out_sems.at[i]).wait()
+
+    def coded(slot):
+        top = jnp.max(jnp.abs(st_ref[...]), axis=(0, 1), keepdims=True)
+        top = jnp.maximum(top, 1e-30)
+        unit_ref[slot] = jnp.broadcast_to(top / 16384.0, (1, 128))
+        stack = st_ref[...]
+        stack = jnp.concatenate([stack[j * here:j * here + 1] for j in range(quads)], axis=0)
+        return encode(stack * (16384.0 / top))
+
+    def one_part(r, hooks):
+        hooks[0]()
         pltpu.make_async_copy(recv.at[r], recv.at[r], recv_sems.at[r]).wait()
 
         @pl.loop(0, ndev, unroll=2)
@@ -125,6 +197,7 @@
             part_ref[d] = fold(data * data)
 
         inv_ref[...] = 1.0 / jnp.sqrt(lane_sum(part_ref) / lags + EPS)
+        hooks[1]()
         tile = 256
 
         @pl.loop(0, lags // tile, unroll=2)
@@ -146,8 +219,10 @@
             ssum = group4(ssum)
             st_ref[:, at] = group4(lin) / days * ((csum * csum + ssum * ssum) / (days * days))
 
-        out = pl.ds(pl.multiple_of(r * rows, rows), rows)
-        pws_ref[out, :] = st_ref[...]
+        code = coded(r)
+        for j in range(4):
+            pws_code[r, j] = code[:, j * width:(j + 1) * width]
+        hooks[2]()
         for step in range(ITERS):
             stack = st_ref[...]
             msq = jnp.sum(fold(stack * stack), axis=1, keepdims=True) / lags
@@ -179,19 +254,68 @@
                     mix = mix + wide(wt_ref[d], chunk) * x32_ref[d, :, at]
                 st_ref[:, at] = group4(mix)
 
-            if step == ITERS - 1:
-                rob_ref[out, :] = st_ref[...] * wide(1.0 / total, lags)
-                lane = lax.broadcasted_iota(jnp.int32, (rows, 128), 1)
-                shares = jnp.zeros((rows, 128), F32)
-                for d in range(ndev):
-                    shares = jnp.where(lane == d, weight[d] / total, shares)
-                w_ref[out, :] = shares
+            if step < ITERS - 1:
+                hooks[3 + step]()
+        st_ref[...] = st_ref[...] * wide(1.0 / total, lags)
+        lane = lax.broadcasted_iota(jnp.int32, (rows, 128), 1)
+        shares = jnp.zeros((rows, 128), F32)
+        for d in range(ndev):
+            shares = jnp.where(lane == d, weight[d] / total, shares)
+        share_ref[pl.ds(pl.multiple_of(r * rows, rows), rows), :] = shares
+        return coded(parts + r)
+
+    def early_part(r, carry):
+        code = one_part(r, [lambda: None] * 5)
+        for j in range(4):
+            rob_code[r, j] = code[:, j * width:(j + 1) * width]
         return carry
 
-    lax.fori_loop(0, parts, one_part, 0)
+    lax.fori_loop(0, early, early_part, 0)
+
+    def each(action, *items):
+        return lambda: [action(i) for i in items]
+
+    def after_phase():
+        forward(0)
+        forward(1)
+        to_lag_group(2)
+
+    code = one_part(early, [each(to_lag_group, 0, 1), each(to_rings, 0, 1), after_phase, each(to_rings, 2), each(forward, 2)])
+
+    lane = lax.broadcasted_iota(jnp.int32, (1, 128), 1)
+    extra = jnp.zeros((1, 128), F32)
+    for j in range(2 * parts):
+        extra = jnp.where(lane == 64 + j, unit_ref[j], extra)
+    row = lax.broadcasted_iota(jnp.int32, (here, 128), 0)
+    words = share_ref[...].T[:ndev]
+    words = jnp.where(lax.broadcasted_iota(jnp.int32, words.shape, 1) < 64, words, extra)
+    high = words.astype(jnp.bfloat16).astype(F32)
+    mid = (words - high).astype(jnp.bfloat16).astype(F32)
+    low = words - high - mid
+    for d in range(ndev):
+        piece = jnp.where(row == 0, high[d:d + 1], jnp.where(row == 1, mid[d:d + 1], low[d:d + 1])).astype(jnp.bfloat16)
+        for j in range(4):
+            tail_code[d, j, :, :width] = code[:, j * width:(j + 1) * width]
+            tail_code[d, j, :, width:] = piece
+
+    def send_tail(k, carry):
+        td, tl = peer(k, me_d, me_l)
+        pltpu.make_async_remote_copy(
+            src_ref=tail_code.at[td, tl], dst_ref=tail_out.at[me_d, me_l],
+            send_sem=tail_sems.at[0], recv_sem=tail_sems.at[1], device_id={"day": td, "lag": tl},
+        ).start()
+        return carry
+
+    lax.fori_loop(1, 64, send_tail, 0)
+    pltpu.make_async_copy(tail_code.at[me_d, me_l], tail_out.at[me_d, me_l], tail_sems.at[1]).start()
     for r in range(parts):
         most = x_ref.at[pl.ds(0, 63 * quads)]
         pltpu.make_async_copy(most, most, send_sem).wait()
+    for i in range(3):
+        finish(i)
+    pltpu.make_async_copy(tail_out, tail_out, tail_sems.at[1]).wait()
+    for part in (tail_code.at[pl.ds(0, ndev - 1)], tail_code.at[ndev - 1, pl.ds(0, 3)]):
+        pltpu.make_async_copy(part, part, tail_sems.at[0]).wait()
 
 
 def stacks(g, x):
@@ -199,85 +323,100 @@
     lags = 4 * width
     parts = 4
     quads = pairs // 64 // parts
-    rows = pairs // 64 * here
     part = quads * here
-    out = jax.ShapeDtypeStruct((rows, lags), F32)
     thin = pltpu.VMEM((16, part, 128), F32)
+    dma = pltpu.SemaphoreType.DMA
+    bf16 = jnp.bfloat16
     return pl.pallas_call(
         functools.partial(stack_kernel, parts),
-        out_shape=(out, out, jax.ShapeDtypeStruct((rows, 128), F32)),
-        in_specs=[VMEM, HBM],
-        out_specs=(VMEM,) * 3,
+        out_shape=(
+            jax.ShapeDtypeStruct((parts, 16, 4, quads, width), bf16),
+            jax.ShapeDtypeStruct((parts - 1, 16, 4, quads, width), bf16),
+            jax.ShapeDtypeStruct((16, 4, quads, width + 128), bf16),
+        ),
+        in_specs=[HBM, HBM],
+        out_specs=(HBM,) * 3,
         scratch_shapes=[
             pltpu.VMEM((parts, 16, quads, here, lags), x.dtype),
-            pltpu.VMEM((lags, lags), jnp.bfloat16),
-            pltpu.VMEM((16, part, lags), jnp.bfloat16),
+            pltpu.VMEM(g.shape, bf16),
+            pltpu.VMEM((lags, lags), bf16),
+            pltpu.VMEM((16, part, lags), bf16),
             pltpu.VMEM((16, part, lags), F32),
             pltpu.VMEM((part, lags), F32),
             thin, thin, thin, thin,
-            pltpu.SemaphoreType.DMA,
-            pltpu.SemaphoreType.DMA((parts,)),
+            pltpu.VMEM((128, 128), F32),
+            pltpu.VMEM((2 * parts, 1, 128), F32),
+            pltpu.VMEM((parts, 4, quads, width), bf16),
+            pltpu.VMEM((parts - 1, 4, quads, width), bf16),
+            pltpu.VMEM((16, 4, quads, width + 128), bf16),
+            dma, dma, dma((parts,)), dma((3,)), dma((3,)), dma((3, 3)), dma((3,)), dma((2,)),
         ],
-        compiler_params=pltpu.CompilerParams(collective_id=0, has_side_effects=True, vmem_limit_bytes=50 * 2**20),
+        compiler_params=pltpu.CompilerParams(collective_id=0, has_side_effects=True, vmem_limit_bytes=63 * 2**20),
         name="stacks",
     )(g, x)
 
 
-def spread_kernel(rows, pws_ref, rob_ref, w_ref, pws_out, rob_out, w_out, send_sems, recv_sems):
-    d = lax.axis_index("day")
-    l = lax.axis_index("lag")
-    entry_barrier(d, l)
-    mine = d * 4 + l
-    at = pl.ds(pl.multiple_of(mine * rows, rows), rows)
-
-    def pairs(td, tl):
-        yield pws_ref.at[tl], pws_out.at[at, :]
-        yield rob_ref.at[tl], rob_out.at[at, :]
-        yield w_ref.at[td], w_out.at[mine]
-
-    def send(k, carry):
-        td, tl = peer(k, d, l)
-        for i, (src, dst) in enumerate(pairs(td, tl)):
-            pltpu.make_async_remote_copy(
-                src_ref=src, dst_ref=dst, send_sem=send_sems.at[i], recv_sem=recv_sems.at[i],
-                device_id={"day": td, "lag": tl},
-            ).start()
-        return carry
-
-    lax.fori_loop(1, 64, send, 0)
-    for i, (src, dst) in enumerate(pairs(d, l)):
-        pltpu.make_async_copy(src, dst, recv_sems.at[i]).start()
-    for i, out in enumerate((pws_out, rob_out, w_out)):
-        pltpu.make_async_copy(out, out, recv_sems.at[i]).wait()
-    for i, most in enumerate((pws_out.at[pl.ds(0, 63 * rows)], rob_out.at[pl.ds(0, 63 * rows)], w_out.at[pl.ds(0, 63)])):
-        pltpu.make_async_copy(most, most, send_sems.at[i]).wait()
-
-
-def spread(pws, rob, w):
-    _, rows, width = pws.shape
-    out = jax.ShapeDtypeStruct((64 * rows, width), F32)
+def decode_kernel(pws_ref, rob_ref, tail_ref, pws_out, rob_out, w_out, words_ref):
+    step = pl.program_id(0)
+    parts, here, _, quads, width = pws_ref.shape
+    count = parts * quads
+    lane = lax.broadcasted_iota(jnp.int32, (count, 128), 1)
+    slot = lax.broadcasted_iota(jnp.int32, (count, 128), 0) // quads + 64
+    for d in range(here):
+        for l in range(4):
+            c = d * 4 + l
+            word = jnp.sum(tail_ref[d, l, :, width:].astype(F32)[:3], axis=0, keepdims=True)
+            words_ref[step * here * 4 + c] = word
+            units = []
+            for base in (0, parts):
+                units.append(jnp.sum(jnp.where(lane == slot + base, word, 0.0), axis=1, keepdims=True))
+            at = slice(c * count, (c + 1) * count)
+            pws_out[at, :] = decode(pws_ref[:, d, l].reshape(count, width)) * units[0]
+            rob = [rob_ref[r, d, l].astype(F32) for r in range(parts - 1)] + [tail_ref[d, l, :, :width].astype(F32)]
+            rob_out[at, :] = decode(jnp.concatenate(rob, axis=0)) * units[1]
+
+    @pl.when(step == pl.num_programs(0) - 1)
+    def _():
+        words = words_ref[...].reshape(64, 128)
+        source = lax.broadcasted_iota(jnp.int32, (128, 128), 0)
+        target = lax.broadcasted_iota(jnp.int32, (128, 128), 1)
+        row = lax.broadcasted_iota(jnp.int32, (64, 128), 0)
+        mine = lax.broadcasted_iota(jnp.int32, (64, 128), 1) // 16 == row % 8
+        for dd in range(w_out.shape[0]):
+            pick = jnp.where(source == target % 16 * 4 + dd, 1.0, 0.0)
+            moved = jnp.dot(words, pick, precision=lax.Precision.HIGHEST, preferred_element_type=F32)
+            moved = jnp.where(mine, moved, 0.0)
+            for j in range(8):
+                w_out[dd:dd + 1, j * 128:(j + 1) * 128] = jnp.sum(moved[j * 8:j * 8 + 8], axis=0, keepdims=True)
+
+
+def decoded(pws, rob, tail):
+    parts, days, _, quads, width = pws.shape
+    here = 4
+    pairs = 64 * parts * quads
+    count = pairs * here // days
+    big = jax.ShapeDtypeStruct((pairs, width), F32)
+    row = pl.BlockSpec((count, width), lambda i: (i, 0))
     return pl.pallas_call(
-        functools.partial(spread_kernel, rows),
-        out_shape=(out, out, jax.ShapeDtypeStruct((64,) + w.shape[1:], F32)),
-        in_specs=[HBM] * 3,
-        out_specs=(HBM,) * 3,
-        scratch_shapes=[pltpu.SemaphoreType.DMA((3,)), pltpu.SemaphoreType.DMA((3,))],
-        compiler_params=pltpu.CompilerParams(collective_id=1, has_side_effects=True),
-        name="spread",
-    )(pws, rob, w)
+        decode_kernel,
+        out_shape=(big, big, jax.ShapeDtypeStruct((4, pairs), F32)),
+        grid=(days // here,),
+        in_specs=[
+            pl.BlockSpec((parts, here, 4, quads, width), lambda i: (0, i, 0, 0, 0)),
+            pl.BlockSpec((parts - 1, here, 4, quads, width), lambda i: (0, i, 0, 0, 0)),
+            pl.BlockSpec((here, 4, quads, width + 128), lambda i: (i, 0, 0, 0)),
+        ],
+        out_specs=(row, row, pl.BlockSpec((4, pairs), lambda i: (0, 0))),
+        scratch_shapes=[pltpu.VMEM((64, 1, 128), F32)],
+        compiler_params=pltpu.CompilerParams(vmem_limit_bytes=63 * 2**20),
+        name="decoded",
+    )(pws, rob, tail)
 
 
 def per_device(corr):
-    pairs, days_here, width = corr.shape
-    lags = width * 4
-    g = jnp.asarray(hilbert_rows(256, lags))
-    pws, rob, w = stacks(g, corr)
-    pws = pws[::4].reshape(16, 4, width).transpose(1, 0, 2)
-    rob = rob[::4].reshape(16, 4, width).transpose(1, 0, 2)
-    w = jnp.broadcast_to(w[:, :16].T.reshape(16, 1, 64), (16, 8, 64))
-    w = jnp.concatenate([w, jnp.zeros_like(w)], axis=2)
-    pws, rob, w = spread(pws, rob, w)
-    return pws, rob, w[:, 0, :64].reshape(pairs, days_here)
+    g = jnp.asarray(hilbert_rows(256, corr.shape[2] * 4))
+    pws, rob, shares = decoded(*stacks(g, corr))
+    return pws, rob, shares.T
 
 
 def solution(mesh):

time: 155 us -> 90.5 us (0.58)
  Pallas kernels: 144 us -> 89.7 us
  local copies, waits for them, and re-layouts: 9.51 us -> 0 us
    pallas_call x2, Pallas kernels: 144 us -> 89.7 us  [the longest x1 84.2 us: stacks(): pl.pallas_call(functools.partial(stack_kernel, parts), out_shape=(jax.Sha...]
    unnamed x7 -> x0, local copies, waits for them, and re-layouts: 6.57 us -> none
where the time goes in v5:
time: 90.5 us; the launch traced here: 90.4 us
  Pallas kernels  89.7 us (99%)
    pallas_call x1, Pallas kernels, stacks(): pl.pallas_call(functools.partial(stack_kernel, parts), out_shape=(jax.Sha...  84.2 us
    pallas_call x1, Pallas kernels, decoded(): pl.pallas_call(decode_kernel, out_shape=(big, big, jax.ShapeDtypeStruct((...  5.52 us

profile of v5, /device:TPU:1, one launch (start us, length us, event | category | flops | bytes accessed | tf_op | source)
XLA Modules:
  0.0 90.4 jit_solution(11821037290208622621)
XLA Ops:
  0.6 84.2 %stacks.1 = (bf16[4,16,4,4,512]{4,3,2,1,0:T(4,128)(2,1)}, bf16[3,16,4,4,512]{4,3,2,1,0:T(4,128)(2,1)}, bf16[16,4,4,640]{3,2,1,0:T(4,128)(2,1)}) custom-call(bf16[256,2048]{1,0:T(8,128)(2,1)} %constant.2.clone.g_ref, bf16[1024,4,512]{2,1,0:T(4,128)(2,1)} %x_ref.1), custom_call_target="tpu_custom_call" | custom-call | tf_op jit(solution)/shard_map/stacks/pallas_call | solution.py:330
  84.9 5.5 %decoded.1 = (f32[1024,512]{1,0:T(8,128)}, f32[1024,512]{1,0:T(8,128)}, f32[4,1024]{1,0:T(4,128)}) custom-call(bf16[4,16,4,4,512]{4,3,2,1,0:T(4,128)(2,1)} %get-tuple-element.9.pws_ref, bf16[3,16,4,4,512]{4,3,2,1,0:T(4,128)(2,1)} %get-tuple-element.10.rob_ref, bf16[16,4,4,640]{3,2,1,0:T(4,128)(2,1)} %get-tuple-element.11.tail_ref), custom_call_target="tpu_custom_call" | custom-call | tf_op jit(solution)/shard_map/decoded/pallas_call | solution.py:400

commit v6 on v5

--- a/solution.py
+++ b/solution.py
@@ -94,7 +94,7 @@
 def stack_kernel(parts, g_ref, x_ref, pws_out, rob_out, tail_out,
                  recv, gv_ref, k_ref, xb_ref, x32_ref, st_ref, part_ref, inv_ref, coh_ref, wt_ref, share_ref, unit_ref,
                  pws_code, rob_code, tail_code,
-                 g_sem, send_sem, recv_sems, out_sems, lag_sems, ring_sems, last_sems, tail_sems):
+                 g_sem, send_sem, recv_sems, out_sems, lag_sems, ring_sems, last_sems, pws_sems, tail_sems):
     me_d = lax.axis_index("day")
     me_l = lax.axis_index("lag")
     ndev, quads, here, lags = recv.shape[1:]
@@ -139,9 +139,9 @@
     lag_peers = [lax.rem(me_l + k, 4) for k in (1, 2, 3)]
     z_peers = [{"day": z_of[k] * 4 + y, "lag": me_l} for k in (1, 3, 2)]
     y_peers = [{"day": z * 4 + y_of[k], "lag": me_l} for k in (1, 3, 2)]
-    first, second = (z_peers, y_peers, z_peers), (y_peers, z_peers, y_peers)
-    codes, outs = (pws_code, rob_code, pws_code), (pws_out, rob_out, pws_out)
-    spans = (pl.ds(0, early), pl.ds(0, early), pl.ds(early, 1))
+    first, second = (z_peers, y_peers) * 2, (y_peers, z_peers) * 2
+    codes, outs = (pws_code, rob_code) * 2, (pws_out, rob_out) * 2
+    spans = (pl.ds(0, early - 1),) * 2 + (pl.ds(early - 1, 1),) * 2
 
     def push(i, src, dst, sem, to):
         pltpu.make_async_remote_copy(
@@ -162,9 +162,10 @@
         for to in second[i]:
             push(i, own, own, last_sems.at[i], to)
 
-    def forward(i):
-        for n, k in enumerate((3, 1, 2)):
-            day = (z_of[k] * 4 + y, z * 4 + y_of[k], z_of[k] * 4 + y)[i]
+    def forward(i, turns):
+        for n in turns:
+            k = (3, 1, 2)[n]
+            day = (z_of[k] * 4 + y, z * 4 + y_of[k])[i % 2]
             got = outs[i].at[spans[i], day]
             pltpu.make_async_copy(got, got, ring_sems.at[i, n]).wait()
             for to in second[i]:
@@ -200,8 +201,7 @@
         hooks[1]()
         tile = 256
 
-        @pl.loop(0, lags // tile, unroll=2)
-        def _(t):
+        def phase(t):
             at = pl.ds(pl.multiple_of(t * tile, tile), tile)
             quad = jnp.dot(xb_ref[...].reshape(ndev * rows, lags), k_ref[:, at], preferred_element_type=F32)
             lin = jnp.zeros((rows, tile), F32)
@@ -219,10 +219,14 @@
             ssum = group4(ssum)
             st_ref[:, at] = group4(lin) / days * ((csum * csum + ssum * ssum) / (days * days))
 
+        half = lags // tile // 2
+        pl.loop(0, half, unroll=2)(phase)
+        hooks[2]()
+        pl.loop(half, 2 * half, unroll=2)(phase)
         code = coded(r)
         for j in range(4):
             pws_code[r, j] = code[:, j * width:(j + 1) * width]
-        hooks[2]()
+        hooks[3]()
         for step in range(ITERS):
             stack = st_ref[...]
             msq = jnp.sum(fold(stack * stack), axis=1, keepdims=True) / lags
@@ -255,7 +259,7 @@
                 st_ref[:, at] = group4(mix)
 
             if step < ITERS - 1:
-                hooks[3 + step]()
+                hooks[4 + step]()
         st_ref[...] = st_ref[...] * wide(1.0 / total, lags)
         lane = lax.broadcasted_iota(jnp.int32, (rows, 128), 1)
         shares = jnp.zeros((rows, 128), F32)
@@ -264,23 +268,46 @@
         share_ref[pl.ds(pl.multiple_of(r * rows, rows), rows), :] = shares
         return coded(parts + r)
 
-    def early_part(r, carry):
-        code = one_part(r, [lambda: None] * 5)
+    def nothing():
+        pass
+
+    def each(action, items, *more):
+        return lambda: [action(i, *more) for i in items]
+
+    def early_part(r, hooks):
+        code = one_part(r, hooks)
         for j in range(4):
             rob_code[r, j] = code[:, j * width:(j + 1) * width]
-        return carry
-
-    lax.fori_loop(0, early, early_part, 0)
-
-    def each(action, *items):
-        return lambda: [action(i) for i in items]
+
+    pl.loop(0, early - 1)(lambda r: early_part(r, [nothing] * 6))
+    early_part(early - 1, [each(to_lag_group, (0, 1)), nothing, nothing, nothing, nothing, each(to_rings, (0, 1))])
+
+    def to_all(src, dst, sems):
+        def send(k, carry):
+            td, tl = peer(k, me_d, me_l)
+            pltpu.make_async_remote_copy(
+                src_ref=src(td, tl), dst_ref=dst, send_sem=sems.at[0], recv_sem=sems.at[1],
+                device_id={"day": td, "lag": tl},
+            ).start()
+            return carry
+
+        lax.fori_loop(1, 64, send, 0)
+        pltpu.make_async_copy(src(me_d, me_l), dst, sems.at[1]).start()
+
+    def last_pws():
+        to_all(lambda td, tl: pws_code.at[early, tl], pws_out.at[early, me_d, me_l], pws_sems)
+
+    def mid_phase():
+        each(to_rings, (2, 3))()
+        each(forward, (0, 1), (0, 1))()
 
     def after_phase():
-        forward(0)
-        forward(1)
-        to_lag_group(2)
-
-    code = one_part(early, [each(to_lag_group, 0, 1), each(to_rings, 0, 1), after_phase, each(to_rings, 2), each(forward, 2)])
+        each(forward, (0, 1), (2,))()
+        last_pws()
+
+    code = one_part(early, [
+        each(to_lag_group, (2, 3)), nothing, mid_phase, after_phase, each(forward, (2, 3), (0, 1)),
+        each(forward, (2, 3), (2,))])
 
     lane = lax.broadcasted_iota(jnp.int32, (1, 128), 1)
     extra = jnp.zeros((1, 128), F32)
@@ -298,21 +325,16 @@
             tail_code[d, j, :, :width] = code[:, j * width:(j + 1) * width]
             tail_code[d, j, :, width:] = piece
 
-    def send_tail(k, carry):
-        td, tl = peer(k, me_d, me_l)
-        pltpu.make_async_remote_copy(
-            src_ref=tail_code.at[td, tl], dst_ref=tail_out.at[me_d, me_l],
-            send_sem=tail_sems.at[0], recv_sem=tail_sems.at[1], device_id={"day": td, "lag": tl},
-        ).start()
-        return carry
-
-    lax.fori_loop(1, 64, send_tail, 0)
-    pltpu.make_async_copy(tail_code.at[me_d, me_l], tail_out.at[me_d, me_l], tail_sems.at[1]).start()
+    to_all(lambda td, tl: tail_code.at[td, tl], tail_out.at[me_d, me_l], tail_sems)
     for r in range(parts):
         most = x_ref.at[pl.ds(0, 63 * quads)]
         pltpu.make_async_copy(most, most, send_sem).wait()
-    for i in range(3):
+    for i in range(4):
         finish(i)
+    last = pws_out.at[early]
+    pltpu.make_async_copy(last, last, pws_sems.at[1]).wait()
+    for part in (last.at[pl.ds(0, ndev - 1)], last.at[ndev - 1, pl.ds(0, 3)]):
+        pltpu.make_async_copy(part, part, pws_sems.at[0]).wait()
     pltpu.make_async_copy(tail_out, tail_out, tail_sems.at[1]).wait()
     for part in (tail_code.at[pl.ds(0, ndev - 1)], tail_code.at[ndev - 1, pl.ds(0, 3)]):
         pltpu.make_async_copy(part, part, tail_sems.at[0]).wait()
@@ -349,7 +371,7 @@
             pltpu.VMEM((parts, 4, quads, width), bf16),
             pltpu.VMEM((parts - 1, 4, quads, width), bf16),
             pltpu.VMEM((16, 4, quads, width + 128), bf16),
-            dma, dma, dma((parts,)), dma((3,)), dma((3,)), dma((3, 3)), dma((3,)), dma((2,)),
+            dma, dma, dma((parts,)), dma((4,)), dma((4,)), dma((4, 3)), dma((4,)), dma((2,)), dma((2,)),
         ],
         compiler_params=pltpu.CompilerParams(collective_id=0, has_side_effects=True, vmem_limit_bytes=63 * 2**20),
         name="stacks",

time: 90.5 us -> 86.8 us (0.959)
  Pallas kernels: 89.7 us -> 86 us
    pallas_call x1, Pallas kernels: 84.2 us -> 80.5 us  [stacks(): pl.pallas_call(functools.partial(stack_kernel, parts), out_shape=(jax.Sha...]
where the time goes in v6:
time: 86.8 us; the launch traced here: 86.7 us
  Pallas kernels  86 us (99%)
    pallas_call x1, Pallas kernels, stacks(): pl.pallas_call(functools.partial(stack_kernel, parts), out_shape=(jax.Sha...  80.5 us
    pallas_call x1, Pallas kernels, decoded(): pl.pallas_call(decode_kernel, out_shape=(big, big, jax.ShapeDtypeStruct((...  5.52 us

profile of v6, /device:TPU:1, one launch (start us, length us, event | category | flops | bytes accessed | tf_op | source)
XLA Modules:
  0.0 86.7 jit_solution(16232950918944725613)
XLA Ops:
  0.6 80.5 %stacks.1 = (bf16[4,16,4,4,512]{4,3,2,1,0:T(4,128)(2,1)}, bf16[3,16,4,4,512]{4,3,2,1,0:T(4,128)(2,1)}, bf16[16,4,4,640]{3,2,1,0:T(4,128)(2,1)}) custom-call(bf16[256,2048]{1,0:T(8,128)(2,1)} %constant.2.clone.g_ref, bf16[1024,4,512]{2,1,0:T(4,128)(2,1)} %x_ref.1), custom_call_target="tpu_custom_call" | custom-call | tf_op jit(solution)/shard_map/stacks/pallas_call | solution.py:352
  81.2 5.5 %decoded.1 = (f32[1024,512]{1,0:T(8,128)}, f32[1024,512]{1,0:T(8,128)}, f32[4,1024]{1,0:T(4,128)}) custom-call(bf16[4,16,4,4,512]{4,3,2,1,0:T(4,128)(2,1)} %get-tuple-element.9.pws_ref, bf16[3,16,4,4,512]{4,3,2,1,0:T(4,128)(2,1)} %get-tuple-element.10.rob_ref, bf16[16,4,4,640]{3,2,1,0:T(4,128)(2,1)} %get-tuple-element.11.tail_ref), custom_call_target="tpu_custom_call" | custom-call | tf_op jit(solution)/shard_map/decoded/pallas_call | solution.py:422

commit v7 on v6

--- a/solution.py
+++ b/solution.py
@@ -15,8 +15,8 @@
 F32 = jnp.float32
 
 
-def hilbert_rows(rows, lags):
-    offset = (np.arange(lags)[None, :] - np.arange(rows)[:, None]) % lags
+def hilbert_matrix(lags):
+    offset = (np.arange(lags)[None, :] - np.arange(lags)[:, None]) % lags
     odd = offset % 2 == 1
     angle = np.pi * offset / lags
     value = np.where(odd, 2.0 / lags * np.cos(angle) / np.where(odd, np.sin(angle), 1.0), 0.0)
@@ -81,7 +81,7 @@
     power = x * x
     power = power * power
     power = power * power
-    return jnp.where(x < 0, -power, power).astype(jnp.bfloat16)
+    return jnp.where(x < 0, -power, power)
 
 
 def decode(code):
@@ -92,7 +92,7 @@
 
 
 def stack_kernel(parts, g_ref, x_ref, pws_out, rob_out, tail_out,
-                 recv, gv_ref, k_ref, xb_ref, x32_ref, st_ref, part_ref, inv_ref, coh_ref, wt_ref, share_ref, unit_ref,
+                 recv, k_ref, xb_ref, x32_ref, st_ref, part_ref, inv_ref, coh_ref, wt_ref, share_ref, unit_ref,
                  pws_code, rob_code, tail_code,
                  g_sem, send_sem, recv_sems, out_sems, lag_sems, ring_sems, last_sems, pws_sems, tail_sems):
     me_d = lax.axis_index("day")
@@ -102,7 +102,7 @@
     days = ndev * here
     width = lags // 4
     early = parts - 1
-    fetch = pltpu.make_async_copy(g_ref, gv_ref, g_sem)
+    fetch = pltpu.make_async_copy(g_ref, k_ref, g_sem)
     fetch.start()
     entry_barrier(me_d, me_l)
     lanes = pl.ds(pl.multiple_of(me_l * width, width), width)
@@ -126,13 +126,6 @@
         pltpu.make_async_copy(block(r, me_d, me_l), recv.at[r, me_d, :, :, lanes], recv_sems.at[r]).start()
 
     fetch.wait()
-    step = g_ref.shape[0]
-    for i in range(lags // step):
-        cut = i * step
-        if cut:
-            k_ref[cut:cut + step, :cut] = gv_ref[:, lags - cut:]
-        k_ref[cut:cut + step, cut:] = gv_ref[:, :lags - cut]
-
     z, y = me_d // 4, lax.rem(me_d, 4)
     z_of = [lax.rem(z + k, 4) for k in range(4)]
     y_of = [lax.rem(y + k, 4) for k in range(4)]
@@ -184,6 +177,10 @@
         stack = st_ref[...]
         stack = jnp.concatenate([stack[j * here:j * here + 1] for j in range(quads)], axis=0)
         return encode(stack * (16384.0 / top))
+
+    def as_tile(code, j):
+        pieces = [code[:, t:t + 128] for t in range(j * width, (j + 1) * width, 128)]
+        return jnp.concatenate(pieces, axis=0).astype(jnp.bfloat16)
 
     def one_part(r, hooks):
         hooks[0]()
@@ -225,7 +222,7 @@
         pl.loop(half, 2 * half, unroll=2)(phase)
         code = coded(r)
         for j in range(4):
-            pws_code[r, j] = code[:, j * width:(j + 1) * width]
+            pws_code[r, j] = as_tile(code, j)
         hooks[3]()
         for step in range(ITERS):
             stack = st_ref[...]
@@ -277,7 +274,7 @@
     def early_part(r, hooks):
         code = one_part(r, hooks)
         for j in range(4):
-            rob_code[r, j] = code[:, j * width:(j + 1) * width]
+            rob_code[r, j] = as_tile(code, j)
 
     pl.loop(0, early - 1)(lambda r: early_part(r, [nothing] * 6))
     early_part(early - 1, [each(to_lag_group, (0, 1)), nothing, nothing, nothing, nothing, each(to_rings, (0, 1))])
@@ -322,7 +319,7 @@
     for d in range(ndev):
         piece = jnp.where(row == 0, high[d:d + 1], jnp.where(row == 1, mid[d:d + 1], low[d:d + 1])).astype(jnp.bfloat16)
         for j in range(4):
-            tail_code[d, j, :, :width] = code[:, j * width:(j + 1) * width]
+            tail_code[d, j, :, :width] = code[:, j * width:(j + 1) * width].astype(jnp.bfloat16)
             tail_code[d, j, :, width:] = piece
 
     to_all(lambda td, tl: tail_code.at[td, tl], tail_out.at[me_d, me_l], tail_sems)
@@ -346,56 +343,59 @@
     parts = 4
     quads = pairs // 64 // parts
     part = quads * here
+    tile = (quads * width // 128, 128)
     thin = pltpu.VMEM((16, part, 128), F32)
     dma = pltpu.SemaphoreType.DMA
     bf16 = jnp.bfloat16
     return pl.pallas_call(
         functools.partial(stack_kernel, parts),
         out_shape=(
-            jax.ShapeDtypeStruct((parts, 16, 4, quads, width), bf16),
-            jax.ShapeDtypeStruct((parts - 1, 16, 4, quads, width), bf16),
+            jax.ShapeDtypeStruct((parts, 16, 4) + tile, bf16),
+            jax.ShapeDtypeStruct((parts - 1, 16, 4) + tile, bf16),
             jax.ShapeDtypeStruct((16, 4, quads, width + 128), bf16),
         ),
         in_specs=[HBM, HBM],
-        out_specs=(HBM,) * 3,
+        out_specs=(VMEM,) * 3,
         scratch_shapes=[
             pltpu.VMEM((parts, 16, quads, here, lags), x.dtype),
             pltpu.VMEM(g.shape, bf16),
-            pltpu.VMEM((lags, lags), bf16),
             pltpu.VMEM((16, part, lags), bf16),
             pltpu.VMEM((16, part, lags), F32),
             pltpu.VMEM((part, lags), F32),
             thin, thin, thin, thin,
             pltpu.VMEM((128, 128), F32),
             pltpu.VMEM((2 * parts, 1, 128), F32),
-            pltpu.VMEM((parts, 4, quads, width), bf16),
-            pltpu.VMEM((parts - 1, 4, quads, width), bf16),
+            pltpu.VMEM((parts, 4) + tile, bf16),
+            pltpu.VMEM((parts - 1, 4) + tile, bf16),
             pltpu.VMEM((16, 4, quads, width + 128), bf16),
             dma, dma, dma((parts,)), dma((4,)), dma((4,)), dma((4, 3)), dma((4,)), dma((2,)), dma((2,)),
         ],
-        compiler_params=pltpu.CompilerParams(collective_id=0, has_side_effects=True, vmem_limit_bytes=63 * 2**20),
+        compiler_params=pltpu.CompilerParams(collective_id=0, has_side_effects=True, vmem_limit_bytes=50 * 2**20),
         name="stacks",
     )(g, x)
 
 
 def decode_kernel(pws_ref, rob_ref, tail_ref, pws_out, rob_out, w_out, words_ref):
     step = pl.program_id(0)
-    parts, here, _, quads, width = pws_ref.shape
-    count = parts * quads
-    lane = lax.broadcasted_iota(jnp.int32, (count, 128), 1)
-    slot = lax.broadcasted_iota(jnp.int32, (count, 128), 0) // quads + 64
+    _, _, quads, width = tail_ref.shape
+    width -= 128
+    here = 4
+    parts = pws_ref.shape[0]
     for d in range(here):
         for l in range(4):
             c = d * 4 + l
-            word = jnp.sum(tail_ref[d, l, :, width:].astype(F32)[:3], axis=0, keepdims=True)
+            word = jnp.sum(tail_ref[step * here + d, l, :, width:].astype(F32)[:3], axis=0, keepdims=True)
             words_ref[step * here * 4 + c] = word
-            units = []
-            for base in (0, parts):
-                units.append(jnp.sum(jnp.where(lane == slot + base, word, 0.0), axis=1, keepdims=True))
-            at = slice(c * count, (c + 1) * count)
-            pws_out[at, :] = decode(pws_ref[:, d, l].reshape(count, width)) * units[0]
-            rob = [rob_ref[r, d, l].astype(F32) for r in range(parts - 1)] + [tail_ref[d, l, :, :width].astype(F32)]
-            rob_out[at, :] = decode(jnp.concatenate(rob, axis=0)) * units[1]
+            for r in range(parts):
+                at = slice((c * parts + r) * quads, (c * parts + r + 1) * quads)
+                for ref, out, slot in ((pws_ref, pws_out, 64 + r), (rob_ref, rob_out, 64 + parts + r)):
+                    unit = word[:, slot:slot + 1]
+                    if r == ref.shape[0]:
+                        out[at, :] = decode(tail_ref[step * here + d, l, :, :width]) * unit
+                        continue
+                    x = decode(ref[r, step * here + d, l]) * unit
+                    for t in range(width // 128):
+                        out[at, t * 128:(t + 1) * 128] = x[t * quads:(t + 1) * quads]
 
     @pl.when(step == pl.num_programs(0) - 1)
     def _():
@@ -413,7 +413,8 @@
 
 
 def decoded(pws, rob, tail):
-    parts, days, _, quads, width = pws.shape
+    parts, days = pws.shape[:2]
+    quads, width = tail.shape[2], tail.shape[3] - 128
     here = 4
     pairs = 64 * parts * quads
     count = pairs * here // days
@@ -423,20 +424,16 @@
         decode_kernel,
         out_shape=(big, big, jax.ShapeDtypeStruct((4, pairs), F32)),
         grid=(days // here,),
-        in_specs=[
-            pl.BlockSpec((parts, here, 4, quads, width), lambda i: (0, i, 0, 0, 0)),
-            pl.BlockSpec((parts - 1, here, 4, quads, width), lambda i: (0, i, 0, 0, 0)),
-            pl.BlockSpec((here, 4, quads, width + 128), lambda i: (i, 0, 0, 0)),
-        ],
+        in_specs=[VMEM] * 3,
         out_specs=(row, row, pl.BlockSpec((4, pairs), lambda i: (0, 0))),
         scratch_shapes=[pltpu.VMEM((64, 1, 128), F32)],
-        compiler_params=pltpu.CompilerParams(vmem_limit_bytes=63 * 2**20),
+        compiler_params=pltpu.CompilerParams(vmem_limit_bytes=40 * 2**20),
         name="decoded",
     )(pws, rob, tail)
 
 
 def per_device(corr):
-    g = jnp.asarray(hilbert_rows(256, corr.shape[2] * 4))
+    g = jnp.asarray(hilbert_matrix(corr.shape[2] * 4))
     pws, rob, shares = decoded(*stacks(g, corr))
     return pws, rob, shares.T
 

time: 86.8 us -> 84.7 us (0.976)
  Pallas kernels: 86 us -> 83.9 us
    pallas_call x1, Pallas kernels: 5.52 us -> 3.8 us  [decoded(): pl.pallas_call(decode_kernel, out_shape=(big, big, jax.ShapeDtypeStruct((...]
where the time goes in v7:
time: 84.7 us; the launch traced here: 84.6 us
  Pallas kernels  83.9 us (99%)
    pallas_call x1, Pallas kernels, stacks(): pl.pallas_call(functools.partial(stack_kernel, parts), out_shape=(jax.Sha...  80.1 us
    pallas_call x1, Pallas kernels, decoded(): pl.pallas_call(decode_kernel, out_shape=(big, big, jax.ShapeDtypeStruct((...  3.8 us

profile of v7, /device:TPU:1, one launch (start us, length us, event | category | flops | bytes accessed | tf_op | source)
XLA Modules:
  0.0 84.6 jit_solution(9713064849414591497)
XLA Ops:
  0.6 80.1 %stacks.1 = (bf16[4,16,4,16,128]{4,3,2,1,0:T(8,128)(2,1)S(1)}, bf16[3,16,4,16,128]{4,3,2,1,0:T(8,128)(2,1)S(1)}, bf16[16,4,4,640]{3,2,1,0:T(4,128)(2,1)S(1)}) custom-call(bf16[2048,2048]{1,0:T(8,128)(2,1)} %constant.2.clone.g_ref, bf16[1024,4,512]{2,1,0:T(4,128)(2,1)} %x_ref.1), custom_call_target="tpu_custom_call" | custom-call | tf_op jit(solution)/shard_map/stacks/pallas_call | solution.py:350
  80.8 3.8 %decoded.1 = (f32[1024,512]{1,0:T(8,128)}, f32[1024,512]{1,0:T(8,128)}, f32[4,1024]{1,0:T(4,128)}) custom-call(bf16[4,16,4,16,128]{4,3,2,1,0:T(8,128)(2,1)S(1)} %get-tuple-element.9.pws_ref, bf16[3,16,4,16,128]{4,3,2,1,0:T(8,128)(2,1)S(1)} %get-tuple-element.10.rob_ref, bf16[16,4,4,640]{3,2,1,0:T(4,128)(2,1)S(1)} %get-tuple-element.11.tail_ref), custom_call_target="tpu_custom_call" | custom-call | tf_op jit(solution)/shard_map/decoded/pallas_call | solution.py:423

commit v8 on v7

--- a/solution.py
+++ b/solution.py
@@ -186,7 +186,7 @@
         hooks[0]()
         pltpu.make_async_copy(recv.at[r], recv.at[r], recv_sems.at[r]).wait()
 
-        @pl.loop(0, ndev, unroll=2)
+        @pl.loop(0, ndev, unroll=4)
         def _(d):
             x = recv[r, d].reshape(rows, lags)
             xb_ref[d] = x
@@ -217,9 +217,9 @@
             st_ref[:, at] = group4(lin) / days * ((csum * csum + ssum * ssum) / (days * days))
 
         half = lags // tile // 2
-        pl.loop(0, half, unroll=2)(phase)
+        pl.loop(0, half, unroll=4)(phase)
         hooks[2]()
-        pl.loop(half, 2 * half, unroll=2)(phase)
+        pl.loop(half, 2 * half, unroll=4)(phase)
         code = coded(r)
         for j in range(4):
             pws_code[r, j] = as_tile(code, j)
@@ -299,8 +299,8 @@
         each(forward, (0, 1), (0, 1))()
 
     def after_phase():
+        last_pws()
         each(forward, (0, 1), (2,))()
-        last_pws()
 
     code = one_part(early, [
         each(to_lag_group, (2, 3)), nothing, mid_phase, after_phase, each(forward, (2, 3), (0, 1)),

time: 84.7 us -> 84.3 us (level)
  no operation moved by 1% of the time
where the time goes in v8:
time: 84.3 us; the launch traced here: 84.2 us
  Pallas kernels  83.6 us (99%)
    pallas_call x1, Pallas kernels, stacks(): pl.pallas_call(functools.partial(stack_kernel, parts), out_shape=(jax.Sha...  79.8 us
    pallas_call x1, Pallas kernels, decoded(): pl.pallas_call(decode_kernel, out_shape=(big, big, jax.ShapeDtypeStruct((...  3.8 us

profile of v8, /device:TPU:1, one launch (start us, length us, event | category | flops | bytes accessed | tf_op | source)
XLA Modules:
  0.0 84.2 jit_solution(14444740979794207559)
XLA Ops:
  0.6 79.8 %stacks.1 = (bf16[4,16,4,16,128]{4,3,2,1,0:T(8,128)(2,1)S(1)}, bf16[3,16,4,16,128]{4,3,2,1,0:T(8,128)(2,1)S(1)}, bf16[16,4,4,640]{3,2,1,0:T(4,128)(2,1)S(1)}) custom-call(bf16[2048,2048]{1,0:T(8,128)(2,1)} %constant.2.clone.g_ref, bf16[1024,4,512]{2,1,0:T(4,128)(2,1)} %x_ref.1), custom_call_target="tpu_custom_call" | custom-call | tf_op jit(solution)/shard_map/stacks/pallas_call | solution.py:350
  80.4 3.8 %decoded.1 = (f32[1024,512]{1,0:T(8,128)}, f32[1024,512]{1,0:T(8,128)}, f32[4,1024]{1,0:T(4,128)}) custom-call(bf16[4,16,4,16,128]{4,3,2,1,0:T(8,128)(2,1)S(1)} %get-tuple-element.9.pws_ref, bf16[3,16,4,16,128]{4,3,2,1,0:T(8,128)(2,1)S(1)} %get-tuple-element.10.rob_ref, bf16[16,4,4,640]{3,2,1,0:T(4,128)(2,1)S(1)} %get-tuple-element.11.tail_ref), custom_call_target="tpu_custom_call" | custom-call | tf_op jit(solution)/shard_map/decoded/pallas_call | solution.py:423
